TPU v7x, 32 devices: a whole 2x2x4 slice. The times are simulated.
32 devices in a mesh: dp: 8 (over z, x), seq: 4 (over y, core).
Axes of the slice: x: 2, y: 2, z: 4, core: 2. Of those that a mesh axis runs over, the one named last changes fastest.
Arguments:
- tokens: bfloat16 [8, 2048, 768], P('dp', 'seq'), may hold values from -6 to 6
- lengths: int32 [8], P('dp'), may hold values from 512 to 2048, as said below
- cotangent: bfloat16 [8, 2048, 768], P('dp', 'seq'), may hold values from -6 to 6
- w_query: bfloat16 [768, 768], replicated, may hold values from -0.21875 to 0.21875
- w_key: bfloat16 [768, 768], replicated, may hold values from -0.21875 to 0.21875
- w_value: bfloat16 [768, 768], replicated, may hold values from -0.21875 to 0.21875
- w_out: bfloat16 [768, 768], replicated, may hold values from -0.875 to 0.875
- w_up: bfloat16 [768, 3072], replicated, may hold values from -0.21875 to 0.21875
- w_down: bfloat16 [3072, 768], replicated, may hold values from -0.109375 to 0.109375
- shared_a: bfloat16 [768, 1024], replicated, may hold values from -0.21875 to 0.21875
- shared_b: bfloat16 [1024, 768], replicated, may hold values from -0.1875 to 0.1875
- vec_biases: float32 [6, 768], replicated, may hold values from -3 to 3
- bias_up: float32 [3072], replicated, may hold values from -3 to 3
- norm_gains: float32 [2, 768], replicated, may hold values from 0.25 to 1.75
- scale_d: float32 [2, 1024], replicated, may hold values from -3 to 3
- scale_b: float32 [2, 768], replicated, may hold values from -3 to 3
- mom_d: float32 [2, 1024], replicated, may hold values from -384 to 384
- sec_d: float32 [2, 1024], replicated, may hold values from 2048 to 32768
- mom_b: float32 [2, 768], replicated, may hold values from -384 to 384
- sec_b: float32 [2, 768], replicated, may hold values from 2048 to 32768
Outputs:
- activations: bfloat16 [8, 2048, 768], P('dp', 'seq')
- grad_input: float32 [8, 2048, 768], P('dp', 'seq')
- moment_d: float32 [2, 1024], replicated
- second_d: float32 [2, 1024], replicated
- moment_b: float32 [2, 768], replicated
- second_b: float32 [2, 768], replicated
- new_d: float32 [2, 1024], replicated
- new_b: float32 [2, 768], replicated
- copy_d: bfloat16 [2, 1024], replicated
- copy_b: bfloat16 [2, 768], replicated
Inputs may be any that keep to these rules, and one draw needn't show every extreme that they name: `lengths`: of the 1 sequence of one index of dp, one holds all 2048 positions; the others hold 512 or more.
All inputs are finite; a program needn't handle non-finite values.
Results may differ from a plain program's by a relative error of at most 0.018.
Values may be sent and summed in bfloat16 or wider, within the bound.
No kernel may reach another device: no remote copies, remote signals or barrier semaphores. Data moves between devices by JAX's collectives and lax.ppermute only.
A program may use at most 192 MiB of HBM per device.

v0:
```python
from functools import partial

import jax
import jax.numpy as jnp
from jax import lax
from jax.sharding import PartitionSpec as P

HEADS = 12
HEAD = 64
STEP = 10


MASKED = -1000000000.0
EPSILON = 1e-05


def product(left, right):
    return jnp.dot(left, right, preferred_element_type=jnp.float32)


def product_back(left, right):
    return lax.dot_general(
        left, right, (((1,), (1,)), ((), ())), preferred_element_type=jnp.float32
    )


def norm_rows(values, gain, shift):
    centred = values - jnp.mean(values, axis=-1, keepdims=True)
    variance = jnp.mean(centred * centred, axis=-1, keepdims=True)
    return centred * lax.rsqrt(variance + EPSILON) * gain + shift


def adamw(weight, moment, second, gradient):
    moment_new = 0.5 * moment + 0.5 * gradient
    second_new = 0.5 * second + 0.5 * gradient * gradient
    first_hat = moment_new / (1.0 - 0.5**STEP)
    second_hat = second_new / (1.0 - 0.5**STEP)
    weight_new = weight - 0.25 * (first_hat / (jnp.sqrt(second_hat) + 1e-08) + 0.01 * weight)
    return (moment_new, second_new, weight_new)


def per_device(
    tokens,
    lengths,
    cotangent,
    w_query,
    w_key,
    w_value,
    w_out,
    w_up,
    w_down,
    shared_a,
    shared_b,
    vec_biases,
    bias_up,
    norm_gains,
    scale_d,
    scale_b,
    mom_d,
    sec_d,
    mom_b,
    sec_b,
):
    f32 = jnp.float32
    bf16 = jnp.bfloat16
    seqs_here, local_len, width = tokens.shape
    n_rows = seqs_here * local_len
    whole_len = local_len * lax.axis_size("seq")
    first_pos = lax.axis_index("seq") * local_len
    shape4 = (seqs_here, local_len, HEADS, HEAD)
    factor = HEAD ** (-0.5)
    inputs = tokens.reshape(n_rows, width)
    latent = product(inputs, shared_a)
    branch_q = product((latent * scale_d[0]).astype(bf16), shared_b)
    branch_v = product((latent * scale_d[1]).astype(bf16), shared_b)
    queries = (
        (product(inputs, w_query) + vec_biases[0] + scale_b[0] * branch_q)
        .astype(bf16)
        .reshape(shape4)
    )
    keys = product(inputs, w_key).astype(bf16).reshape(seqs_here, local_len, width)
    values = (
        (product(inputs, w_value) + vec_biases[1] + scale_b[1] * branch_v)
        .astype(bf16)
        .reshape(seqs_here, local_len, width)
    )
    start_carry = (
        jnp.full(shape4[:3], -1e30, f32),
        jnp.zeros(shape4[:3], f32),
        jnp.zeros(shape4, f32),
    )
    pieces = (
        lax.all_gather(keys, "seq", axis=1, tiled=True),
        lax.all_gather(values, "seq", axis=1, tiled=True),
    )

    def per_sequence(items):
        query_s, key_s, value_s, count, top, total, accum = items
        key_h = key_s.reshape(-1, HEADS, HEAD)
        value_h = value_s.reshape(-1, HEADS, HEAD)
        scores = jnp.einsum("qhd,khd->qhk", query_s, key_h, preferred_element_type=f32) * factor
        usable = jnp.arange(key_h.shape[0], dtype=jnp.int32) < count
        scores = jnp.where(usable[None, None, :], scores, MASKED)
        top_new = jnp.maximum(top, jnp.max(scores, axis=-1))
        rescale = jnp.exp(top - top_new)
        weights = jnp.exp(scores - top_new[..., None])
        total_new = total * rescale + jnp.sum(weights, axis=-1)
        accum_new = accum * rescale[..., None] + jnp.einsum(
            "qhk,khd->qhd", weights.astype(bf16), value_h, preferred_element_type=f32
        )
        return (top_new, total_new, accum_new)

    top, total, accum = lax.map(
        per_sequence,
        (queries, pieces[0], pieces[1], lengths, start_carry[0], start_carry[1], start_carry[2]),
    )
    context = accum / total[..., None]
    log_total = top + jnp.log(total)
    context_low = context.astype(bf16).reshape(n_rows, width)
    attn_out = product(context_low, w_out) + vec_biases[2]
    first_sum = inputs.astype(f32) + attn_out
    normed, norm_one_back = jax.vjp(
        lambda vals: norm_rows(vals, norm_gains[0], vec_biases[4]), first_sum
    )
    pre_act = product(normed.astype(bf16), w_up) + bias_up
    hidden, gelu_back = jax.vjp(partial(jax.nn.gelu, approximate=False), pre_act)
    ffn_out = product(hidden.astype(bf16), w_down) + vec_biases[3]
    result, norm_two_back = jax.vjp(
        lambda vals: norm_rows(vals, norm_gains[1], vec_biases[5]), normed + ffn_out
    )
    positions = first_pos + jnp.arange(local_len, dtype=jnp.int32)
    row_mask = (positions[None, :] < lengths[:, None]).astype(f32).reshape(n_rows, 1)
    activations = (result * row_mask).astype(bf16).reshape(tokens.shape)
    grad_result = cotangent.astype(f32).reshape(n_rows, width) * row_mask
    grad_second = norm_two_back(grad_result)[0]
    grad_hidden = product_back(grad_second.astype(bf16), w_down)
    grad_pre = gelu_back(grad_hidden)[0].astype(bf16)
    grad_normed = grad_second + product_back(grad_pre, w_up)
    grad_first = norm_one_back(grad_normed)[0]
    grad_context = product_back(grad_first.astype(bf16), w_out).astype(bf16).reshape(shape4)
    delta_rows = jnp.sum(grad_context.astype(f32) * context, axis=-1)
    back_carry = (
        jnp.zeros(shape4, f32),
        jnp.zeros((seqs_here, whole_len, width), f32),
        jnp.zeros((seqs_here, whole_len, width), f32),
    )
    pieces = (
        lax.all_gather(keys, "seq", axis=1, tiled=True),
        lax.all_gather(values, "seq", axis=1, tiled=True),
    )

    def per_sequence(items):
        (
            query_s,
            key_s,
            value_s,
            count,
            lse_s,
            delta_s,
            grad_ctx_s,
            grad_q,
            grad_k_all,
            grad_v_all,
        ) = items
        key_h = key_s.reshape(-1, HEADS, HEAD)
        value_h = value_s.reshape(-1, HEADS, HEAD)
        scores = jnp.einsum("qhd,khd->qhk", query_s, key_h, preferred_element_type=f32) * factor
        usable = jnp.arange(key_h.shape[0], dtype=jnp.int32) < count
        scores = jnp.where(usable[None, None, :], scores, MASKED)
        probs = jnp.exp(scores - lse_s[..., None])
        grad_probs = jnp.einsum("qhd,khd->qhk", grad_ctx_s, value_h, preferred_element_type=f32)
        grad_scores = (probs * (grad_probs - delta_s[..., None])).astype(bf16)
        grad_q_new = grad_q + factor * jnp.einsum(
            "qhk,khd->qhd", grad_scores, key_h, preferred_element_type=f32
        )
        key_grad = factor * jnp.einsum(
            "qhk,qhd->khd", grad_scores, query_s, preferred_element_type=f32
        )
        value_grad = jnp.einsum(
            "qhk,qhd->khd", probs.astype(bf16), grad_ctx_s, preferred_element_type=f32
        )
        grad_k_all = key_grad.reshape(-1, width)
        grad_v_all = value_grad.reshape(-1, width)
        return (grad_q_new, grad_k_all, grad_v_all)

    grad_q, grad_k_all, grad_v_all = lax.map(
        per_sequence,
        (
            queries,
            pieces[0],
            pieces[1],
            lengths,
            log_total,
            delta_rows,
            grad_context,
            back_carry[0],
            back_carry[1],
            back_carry[2],
        ),
    )
    grad_k_own, grad_v_own = (
        lax.psum_scatter(
            grad_k_all.astype(jnp.bfloat16), "seq", scatter_dimension=1, tiled=True
        ).astype(jnp.float32),
        lax.psum_scatter(
            grad_v_all.astype(jnp.bfloat16), "seq", scatter_dimension=1, tiled=True
        ).astype(jnp.float32),
    )
    grad_q_low = grad_q.reshape(n_rows, width).astype(bf16)
    grad_k_low = grad_k_own.reshape(n_rows, width).astype(bf16)
    grad_v_low = grad_v_own.reshape(n_rows, width).astype(bf16)
    grad_q_wide = grad_q_low.astype(f32)
    grad_v_wide = grad_v_low.astype(f32)
    grad_branch_q = (scale_b[0] * grad_q_wide).astype(bf16)
    grad_branch_v = (scale_b[1] * grad_v_wide).astype(bf16)
    total_b = jnp.stack(
        [jnp.sum(branch_q * grad_q_wide, axis=0), jnp.sum(branch_v * grad_v_wide, axis=0)]
    )
    grad_lat_q = product_back(grad_branch_q, shared_b)
    grad_lat_v = product_back(grad_branch_v, shared_b)
    total_d = jnp.stack(
        [jnp.sum(latent * grad_lat_q, axis=0), jnp.sum(latent * grad_lat_v, axis=0)]
    )
    grad_latent = (grad_lat_q * scale_d[0] + grad_lat_v * scale_d[1]).astype(bf16)
    grad_inputs = grad_first + product_back(grad_q_low, w_query) + product_back(grad_k_low, w_key)
    grad_inputs = (
        grad_inputs + product_back(grad_v_low, w_value) + product_back(grad_latent, shared_a)
    )
    total_d, total_b = lax.psum((total_d, total_b), ("dp", "seq"))
    moment_d, second_d, new_d = adamw(scale_d, mom_d, sec_d, total_d)
    moment_b, second_b, new_b = adamw(scale_b, mom_b, sec_b, total_b)
    return (
        activations,
        grad_inputs.reshape(tokens.shape),
        moment_d,
        second_d,
        moment_b,
        second_b,
        new_d,
        new_b,
        new_d.astype(bf16),
        new_b.astype(bf16),
    )


def solution(mesh):
    placed = (
        P("dp", "seq", None),
        P("dp"),
        P("dp", "seq", None),
        P(),
        P(),
        P(),
        P(),
        P(),
        P(),
        P(),
        P(),
        P(),
        P(),
        P(),
        P(),
        P(),
        P(),
        P(),
        P(),
        P(),
    )
    return jax.shard_map(
        per_device,
        mesh=mesh,
        in_specs=placed,
        out_specs=(
            P("dp", "seq", None),
            P("dp", "seq", None),
            P(),
            P(),
            P(),
            P(),
            P(),
            P(),
            P(),
            P(),
        ),
        check_vma=False,
    )
```

profile of v0, /device:TPU:0, one launch (start us, length us, event | category | flops | bytes accessed | tf_op | source)
XLA Modules:
  0.0 320.7 jit_solution(16158211401626597364)
XLA Ops:
  7.3 3.3 %convolution_convert_fusion.1 = bf16[512,768]{1,0:T(8,128)(2,1)} fusion(bf16[768,768]{1,0:T(8,128)(2,1)} %param.24, bf16[1,512,768]{2,1,0:T(8,128)(2,1)} %param.20), kind=kOutput, calls=%fused_computation.77 | convolution fusion | flops 604372992 | bytes 2752512 | tf_op jit(solution)/shard_map/dot_general | solution.py:18
  10.9 2.1 fusion.58
  13.0 1.0 fusion.39
  14.0 0.3 copy-done.1
  14.3 1.1 copy-done.6
  15.5 1.7 add_convert_fusion.3
  17.2 0.3 reduce-scatter.5.cloned.1.call-start
  17.5 2.7 fusion.38
  20.2 1.2 copy-done.7
  21.4 0.8 add_convert_fusion.4
  22.2 0.3 copy.44
  23.2 18.8 %all-gather.5.cloned.1.call-done = bf16[2048,768]{1,0:T(8,128)(2,1)} async-done(((bf16[512,768]{1,0:T(8,128)(2,1)}), bf16[2048,768]{1,0:T(8,128)(2,1)}) %all-gather.5.cloned.1.call-update) | async-done | bytes 3145744 | tf_op jit(solution)/shard_map/all_gather | solution.py:93
  42.0 4.7 %copy.43 = bf16[2048,768]{0,1:T(8,128)(2,1)} copy(bf16[2048,768]{1,0:T(8,128)(2,1)} %all-gather.5.cloned.1.call-done) | data formatting | bytes 6291456 | tf_op jit(solution)/shard_map/all_gather | solution.py:93
  46.7 20.5 %bitcast_reduce_fusion = (f32[512,12]{0,1:T(8,128)S(1)}, f32[12,2048,512]{2,1,0:T(8,128)}) fusion(pred[2048]{0:T(1024)(128)(4,1)S(1)} %iota_compare_fusion, bf16[2048,12,64]{0,2,1:T(8,128)(2,1)} %bitcast.115, bf16[512,12,64]{0,2,1:T(8,128)(2,1)S(1)} %bitcast.118), kind=kOutput, calls=%fused_computation.5 | convolution fusion | flops 1648355328 | bytes 54290432 | tf_op jit(solution)/shard_map/while/body/eval_jaxpr/qhd,khd->qhk/dot_general | solution.py:101
  67.3 22.0 %fusion.5 = f32[512,12]{0,1:T(8,128)S(1)} fusion(f32[12,2048,512]{2,1,0:T(8,128)} %get-tuple-element.104, f32[512,12]{0,1:T(8,128)S(1)} %broadcast_maximum_fusion, pred[2048]{0:T(1024)(128)(4,1)S(1)} %iota_compare_fusion), kind=kLoop, calls=%fused_computation.10 | loop fusion | flops 50325504 | bytes 50382848 | tf_op jit(solution)/shard_map/while/body/eval_jaxpr/reduce_sum | solution.py:107
  89.4 4.7 %copy.45 = bf16[2048,768]{0,1:T(8,128)(2,1)} copy(bf16[2048,768]{1,0:T(8,128)(2,1)} %all-gather.7.cloned.1.call-done) | data formatting | bytes 6291456 | tf_op jit(solution)/shard_map/all_gather | solution.py:94
  94.1 21.7 %fusion.92 = (bf16[512,12,64]{0,2,1:T(8,128)(2,1)S(1)}, f32[512,12,64]{0,2,1:T(8,128)}) fusion(f32[512,12]{0,1:T(8,128)S(1)} %get-tuple-element.97, bf16[2048,12,64]{0,2,1:T(8,128)(2,1)} %bitcast.120, f32[12,2048,512]{2,1,0:T(8,128)} %get-tuple-element.104, f32[512,12]{0,1:T(8,128)S(1)} %broadcast_maximum_fusion, ...), kind=kOutput, calls=%fused_computation.158 | convolution fusion | flops 1662124032 | bytes 55912448 | tf_op jit(solution)/shard_map/while/body/eval_jaxpr/qhk,khd->qhd/dot_general | solution.py:108
  115.9 0.9 fusion.93
  116.8 0.3 multiply_reduce_fusion.5
  117.2 17.8 %fusion.13 = (f32[512,3072]{1,0:T(8,128)S(1)}, f32[512,3072]{1,0:T(8,128)S(1)}) fusion(f32[3072]{0:T(1024)S(1)} %copy-done.39, bf16[768,3072]{1,0:T(8,128)(2,1)} %param.27, f32[512,768]{1,0:T(8,128)S(1)} %get-tuple-element.108, f32[768]{0:T(1024)S(1)} %get-tuple-element.61, f32[768]{0:T(1024)S(1)} %get-tuple-element.78, f32[512]{0:T(512)S(1)} %fusion.74, ...), kind=kOutput, calls=%fused_computation.17 | convolution fusion | flops 2516975616 | bytes 18896896 | tf_op jit(solution)/shard_map/dot_general | solution.py:18
  135.1 2.9 fusion.94
  138.0 1.5 copy-done.41
  139.5 0.7 fusion.33
  140.2 2.2 fusion.90
  142.5 15.0 %multiply_reduce_fusion.3 = (f32[512]{0:T(512)S(1)}, f32[512,768]{1,0:T(8,128)}) fusion(f32[512,768]{1,0:T(8,128)S(1)} %get-tuple-element.108, f32[512]{0:T(512)S(1)} %broadcast_multiply_fusion.1, f32[768]{0:T(1024)S(1)} %get-tuple-element.78, bf16[768,3072]{1,0:T(8,128)(2,1)} %param.27, f32[512,3072]{1,0:T(8,128)} %copy-done.40, ...), kind=kOutput, calls=%fused_computation.64 | convolution fusion | flops 4858576384 | bytes 26760192 | tf_op jit(solution)/shard_map/dot_general | solution.py:22
  157.5 2.0 fusion.89
  159.5 1.1 copy-done.8
  160.7 0.8 convolution_convert_fusion
  161.5 0.3 copy.47
  161.8 21.4 %fusion.19 = bf16[12,64,2048]{2,1,0:T(8,128)(2,1)} fusion(bf16[512,12,64]{0,2,1:T(8,128)(2,1)S(1)} %bitcast.123, f32[12,2048,512]{2,1,0:T(8,128)} %get-tuple-element.104, f32[512,12]{0,1:T(8,128)S(1)} %get-tuple-element.96, pred[2048]{0:T(1024)(128)(4,1)S(1)} %iota_compare_fusion), kind=kOutput, calls=%fused_computation.34 | convolution fusion | flops 1662517248 | bytes 54290432 | tf_op jit(solution)/shard_map/while/body/eval_jaxpr/qhk,qhd->khd/dot_general | solution.py:179
  183.2 4.7 %copy.51 = bf16[1,2048,768]{2,1,0:T(8,128)(2,1)} copy(bf16[1,2048,768]{1,2,0:T(8,128)(2,1)} %bitcast.122) | data formatting | bytes 6291456 | tf_op jit(solution)/shard_map/convert_element_type | solution.py:206
  188.0 1.7 multiply_reduce_fusion.2
  189.7 32.4 %fusion.1 = bf16[512,12,2048]{0,2,1:T(8,128)(2,1)} fusion(f32[12,2048,512]{2,1,0:T(8,128)} %get-tuple-element.104, f32[512,12]{0,1:T(8,128)S(1)} %multiply_reduce_fusion.2, f32[512,12]{0,1:T(8,128)S(1)} %get-tuple-element.96, pred[2048]{0:T(1024)(128)(4,1)S(1)} %iota_compare_fusion, bf16[2048,12,64]{0,2,1:T(8,128)(2,1)} %bitcast.121, ...), kind=kOutput, calls=%fused_computation.2 | convolution fusion | flops 1686110208 | bytes 79480832 | tf_op jit(solution)/shard_map/while/body/eval_jaxpr/qhd,khd->qhk/dot_general | solution.py:171
  222.1 13.8 %multiply_convert_fusion = bf16[12,64,2048]{2,1,0:T(8,128)(2,1)} fusion(bf16[512,12,64]{0,2,1:T(8,128)(2,1)S(1)} %bitcast.119, bf16[512,12,2048]{0,2,1:T(8,128)(2,1)} %fusion.1), kind=kOutput, calls=%fused_computation.18 | convolution fusion | flops 1613758464 | bytes 29097984 | tf_op jit(solution)/shard_map/while/body/eval_jaxpr/qhk,qhd->khd/dot_general | solution.py:176
  235.9 14.8 %multiply_convert_fusion.5 = bf16[12,64,512]{2,1,0:T(8,128)(2,1)S(1)} fusion(bf16[2048,12,64]{0,2,1:T(8,128)(2,1)} %bitcast.116, bf16[512,12,2048]{0,2,1:T(8,128)(2,1)} %fusion.1), kind=kOutput, calls=%fused_computation.62 | convolution fusion | flops 1611399168 | bytes 29097984 | tf_op jit(solution)/shard_map/while/body/eval_jaxpr/qhk,khd->qhd/dot_general | solution.py:173
  250.7 0.3 copy.52
  251.0 1.7 fusion.27
  252.8 2.0 fusion.95
  254.8 1.9 fusion.29
  256.7 1.0 fusion.49
  257.8 0.5 copy-done.2
  258.4 2.4 multiply_reduce_fusion.1
  260.9 40.1 %all-reduce = (f32[2,1024]{1,0:T(2,128)S(1)}, f32[2,768]{1,0:T(2,128)S(1)}) all-reduce(f32[2,1024]{1,0:T(2,128)S(1)} %pad_maximum_fusion, f32[2,768]{1,0:T(2,128)S(1)} %pad_maximum_fusion.1), channel_id=1, replica_groups=mesh['dp'=8,'seq'=4] {'dp','seq'}, use_global_device_ids=true, to_apply=%region_15.16 | all-reduce | flops 3584 | bytes 28672 | tf_op jit(solution)/shard_map/psum | solution.py:229
  301.0 0.6 fusion.85
  301.6 0.6 fusion.87
  302.2 4.9 %fusion.40 = f32[512,768]{1,0:T(8,128)} fusion(bf16[768,1024]{1,0:T(8,128)(2,1)} %param.29, f32[512,1024]{1,0:T(8,128)} %copy-done.5, f32[512,1024]{1,0:T(8,128)} %get-tuple-element.115, f32[1024]{0:T(1024)S(1)} %bitcast.131, f32[1024]{0:T(1024)S(1)} %bitcast.129), kind=kOutput, calls=%fused_computation.81 | convolution fusion | flops 807403520 | bytes 7348224 | tf_op jit(solution)/shard_map/dot_general | solution.py:22
  307.1 2.5 fusion.55
  309.6 4.1 %add_bitcast_fusion = f32[1,512,768]{2,1,0:T(8,128)} fusion(f32[512,768]{1,0:T(8,128)S(1)} %copy-done.10, f32[512,768]{1,0:T(8,128)S(1)} %fusion.55, f32[512,768]{1,0:T(8,128)} %fusion.95, bf16[768,768]{1,0:T(8,128)(2,1)} %param.25, f32[512,768]{1,0:T(8,128)S(1)} %copy-done.9, bf16[1,512,768]{2,1,0:T(8,128)(2,1)} %reduce-scatter.5.cloned.1.call-done, ...), kind=kOutput, calls=%fused_computation.61 | convolution fusion | flops 605945856 | bytes 9832448 | tf_op jit(solution)/shard_map/dot_general | solution.py:22
  (111 shorter events, 0.7 us)
Async XLA Ops:
  7.2 5.8 %copy-start = (bf16[1024,768]{1,0:T(8,128)(2,1)S(1)}, bf16[1024,768]{1,0:T(8,128)(2,1)}, u32[]{:S(2)}) copy-start(bf16[1024,768]{1,0:T(8,128)(2,1)} %param.30) | copy-start | bytes 4718596
  7.2 3.5 %copy-start.25 = (f32[6,768]{1,0:T(8,128)S(1)}, f32[6,768]{1,0:T(8,128)}, u32[]{:S(2)}) copy-start(f32[6,768]{1,0:T(8,128)} %param.31) | copy-start | bytes 55300
  7.2 3.5 %copy-start.21 = (f32[2,768]{1,0:T(2,128)S(1)}, f32[2,768]{1,0:T(2,128)}, u32[]{:S(2)}) copy-start(f32[2,768]{1,0:T(2,128)} %param.35) | copy-start | bytes 18436
  7.2 3.6 %copy-start.19 = (f32[2,1024]{1,0:T(2,128)S(1)}, f32[2,1024]{1,0:T(2,128)}, u32[]{:S(2)}) copy-start(f32[2,1024]{1,0:T(2,128)} %param.34) | copy-start | bytes 24580
  7.2 3.6 %copy-start.13 = (bf16[768,1024]{1,0:T(8,128)(2,1)S(1)}, bf16[768,1024]{1,0:T(8,128)(2,1)}, u32[]{:S(2)}) copy-start(bf16[768,1024]{1,0:T(8,128)(2,1)} %param.29) | copy-start | bytes 4718596
  7.2 34.8 %all-gather.5.cloned.1.call-start = ((), (), s32[]{:S(2)}) async-start(), calls=%async_computation.4 | async-start | bytes 3932160 | tf_op jit(solution)/shard_map/all_gather | solution.py:93
  10.6 78.7 %all-gather.7.cloned.1.call-start = ((), (), s32[]{:S(2)}) async-start(), calls=%async_computation.5 | async-start | bytes 3932160 | tf_op jit(solution)/shard_map/all_gather | solution.py:94
  10.8 3.6 %copy-start.31 = (f32[768]{0:T(1024)}, f32[768]{0:T(1024)S(1)}, u32[]{:S(2)}) copy-start(f32[768]{0:T(1024)S(1)} %get-tuple-element.116) | copy-start | bytes 9220
  10.8 9.4 %copy-start.23 = (f32[768]{0:T(1024)}, f32[768]{0:T(1024)S(1)}, u32[]{:S(2)}) copy-start(f32[768]{0:T(1024)S(1)} %get-tuple-element.117) | copy-start | bytes 9220
  10.8 2.2 copy-start.17
  10.8 6.6 %copy-start.15 = (f32[1,1024]{1,0:T(1,128)}, f32[1,1024]{1,0:T(1,128)S(1)}, u32[]{:S(2)}) copy-start(f32[1,1024]{1,0:T(1,128)S(1)} %get-tuple-element.99) | copy-start | bytes 12292
  13.0 1.4 copy-start.1
  13.0 2.5 copy-start.14
  13.0 2.5 copy-start.37
  14.3 1.1 copy-start.6
  17.2 237.6 %reduce-scatter.5.cloned.1.call-start = ((), (), s32[]{:S(2)}) async-start(), calls=%async_computation.3 | async-start | bytes 3932160 | tf_op jit(solution)/shard_map/reduce_scatter | solution.py:205
  17.5 3.9 %copy-start.35 = (bf16[768,768]{1,0:T(8,128)(2,1)S(1)}, bf16[768,768]{1,0:T(8,128)(2,1)}, u32[]{:S(2)}) copy-start(bf16[768,768]{1,0:T(8,128)(2,1)} %param.23) | copy-start | bytes 3538948
  20.2 1.2 copy-start.7
  21.4 1.8 copy-start.28
  22.5 24.3 %copy-start.3 = (bf16[512,768]{0,1:T(8,128)(2,1)}, bf16[512,768]{0,1:T(8,128)(2,1)S(1)}, u32[]{:S(2)}) copy-start(bf16[512,768]{0,1:T(8,128)(2,1)S(1)} %copy.44) | copy-start | bytes 2359300
  94.1 21.8 %copy-start.33 = (bf16[768,768]{1,0:T(8,128)(2,1)S(1)}, bf16[768,768]{1,0:T(8,128)(2,1)}, u32[]{:S(2)}) copy-start(bf16[768,768]{1,0:T(8,128)(2,1)} %param.26) | copy-start | bytes 3538948
  94.1 21.8 %copy-start.38 = (bf16[1,512,768]{2,1,0:T(8,128)(2,1)S(1)}, bf16[1,512,768]{2,1,0:T(8,128)(2,1)}, u32[]{:S(2)}) copy-start(bf16[1,512,768]{2,1,0:T(8,128)(2,1)} %param.20) | copy-start | bytes 2359300
  115.9 1.3 copy-start.39
  115.9 19.1 %slice-start = ((s8[4718592]{0:T(1024)(128)(4,1)}), s8[4194304]{0:T(1024)(128)(4,1)S(1)}, s32[]{:S(2)}) async-start(s8[4718592]{0:T(1024)(128)(4,1)} %bitcast.134), calls=%async_computation.6 | async-start | bytes 8388608
  117.2 17.9 %slice-start.1 = ((s8[4718592]{0:T(1024)(128)(4,1)}), s8[524288]{0:T(1024)(128)(4,1)S(1)}, s32[]{:S(2)}) async-start(s8[4718592]{0:T(1024)(128)(4,1)} %bitcast.134), calls=%async_computation.7 | async-start | bytes 1048576
  135.0 3.0 copy-start.40
  135.0 4.5 %copy-start.41 = (f32[512,3072]{1,0:T(8,128)}, f32[512,3072]{1,0:T(8,128)S(1)}, u32[]{:S(2)}) copy-start(f32[512,3072]{1,0:T(8,128)S(1)} %get-tuple-element.110) | copy-start | bytes 18874372
  135.0 4.4 %copy-start.11 = (bf16[1,512,768]{2,1,0:T(8,128)(2,1)S(1)}, bf16[1,512,768]{2,1,0:T(8,128)(2,1)}, u32[]{:S(2)}) copy-start(bf16[1,512,768]{2,1,0:T(8,128)(2,1)} %param.22) | copy-start | bytes 2359300
  157.5 3.2 copy-start.34
  159.5 1.2 copy-start.8
  187.9 119.2 %reduce-scatter.3.cloned.1.call-start = ((), (), s32[]{:S(2)}) async-start(), calls=%async_computation.2 | async-start | bytes 3932160 | tf_op jit(solution)/shard_map/reduce_scatter | solution.py:202
  189.7 32.4 %copy-start.4 = (bf16[512,768]{0,1:T(8,128)(2,1)S(1)}, bf16[512,768]{0,1:T(8,128)(2,1)}, u32[]{:S(2)}) copy-start(bf16[512,768]{0,1:T(8,128)(2,1)} %copy-done.3) | copy-start | bytes 2359300
  251.0 1.7 copy-start.36
  254.8 1.9 copy-start.32
  254.8 1.9 copy-start.12
  256.7 1.6 copy-start.2
  256.7 1.6 copy-start.24
  258.3 2.5 copy-start.5
  258.3 42.6 %copy-start.22 = (f32[2,768]{1,0:T(2,128)S(1)}, f32[2,768]{1,0:T(2,128)}, u32[]{:S(2)}) copy-start(f32[2,768]{1,0:T(2,128)} %param.35) | copy-start | bytes 18436
  258.3 42.6 %copy-start.29 = (f32[2,768]{1,0:T(2,128)S(1)}, f32[2,768]{1,0:T(2,128)}, u32[]{:S(2)}) copy-start(f32[2,768]{1,0:T(2,128)} %param.39) | copy-start | bytes 18436
  258.3 42.6 %copy-start.30 = (f32[2,768]{1,0:T(2,128)S(1)}, f32[2,768]{1,0:T(2,128)}, u32[]{:S(2)}) copy-start(f32[2,768]{1,0:T(2,128)} %param.38) | copy-start | bytes 18436
  258.3 43.2 %copy-start.20 = (f32[2,1024]{1,0:T(2,128)S(1)}, f32[2,1024]{1,0:T(2,128)}, u32[]{:S(2)}) copy-start(f32[2,1024]{1,0:T(2,128)} %param.34) | copy-start | bytes 24580
  258.3 43.2 %copy-start.26 = (f32[2,1024]{1,0:T(2,128)S(1)}, f32[2,1024]{1,0:T(2,128)}, u32[]{:S(2)}) copy-start(f32[2,1024]{1,0:T(2,128)} %param.37) | copy-start | bytes 24580
  258.4 43.2 %copy-start.27 = (f32[2,1024]{1,0:T(2,128)S(1)}, f32[2,1024]{1,0:T(2,128)}, u32[]{:S(2)}) copy-start(f32[2,1024]{1,0:T(2,128)} %param.36) | copy-start | bytes 24580
  258.4 43.9 %copy-start.16 = (f32[1,1024]{1,0:T(1,128)S(1)}, f32[1,1024]{1,0:T(1,128)}, u32[]{:S(2)}) copy-start(f32[1,1024]{1,0:T(1,128)} %copy-done.15) | copy-start | bytes 12292
  258.4 43.9 %copy-start.18 = (f32[1,1024]{1,0:T(1,128)S(1)}, f32[1,1024]{1,0:T(1,128)}, u32[]{:S(2)}) copy-start(f32[1,1024]{1,0:T(1,128)} %copy-done.17) | copy-start | bytes 12292
  307.1 2.5 copy-start.9
  307.1 2.5 copy-start.10
Sparse Core Ops, SparseCore 0:
  10.7 31.2 all-gather.4
  44.1 28.5 all-gather.6
  188.0 38.3 reduce-scatter.4
  236.0 38.8 reduce-scatter.2
where the time goes:
time: 324 us; the launch traced here: 321 us
  matrix products  191 us (59%)
  blocking collectives  40.1 us (12%)
  other arithmetic  34 us (10%)
  local copies, waits for them, and re-layouts  21.1 us (7%)
  waiting for transfers between devices  18.9 us (6%)
  between operations  15.5 us (5%)
    psum x1, blocking collectives, per_device(): total_d, total_b = lax.psum((total_d, total_b), ('dp', 'seq'))  40.1 us
    dot_general x9, matrix products, product(): return jnp.dot(left, right, preferred_element_type=jnp.float32)  33.3 us
    dot_general x8, matrix products, product_back(): lax.dot_general(left, right, (((1,), (1,)), ((), ())), preferred_element_...  32.8 us
    dot_general x1, matrix products, per_sequence(): jnp.einsum('qhd,khd->qhk', grad_ctx_s, value_h, preferred_element_type=f32)  32.4 us
    reduce_sum x1, other arithmetic, per_sequence(): total_new = total * rescale + jnp.sum(weights, axis=-1)  22 us
    dot_general x1, matrix products, per_sequence(): jnp.einsum('qhk,khd->qhd', weights.astype(bf16), value_h, preferred_eleme...  21.7 us
    dot_general x1, matrix products, per_sequence(): jnp.einsum('qhk,qhd->khd', probs.astype(bf16), grad_ctx_s, preferred_elem...  21.4 us
    dot_general x1, matrix products, per_sequence(): jnp.einsum('qhd,khd->qhk', query_s, key_h, preferred_element_type=f32)  20.5 us
  transfers between devices with their start and end apart: 4, of which 1 were waited for; matrix products, arithmetic and copies ran while one was open for 42% of the time, Pallas kernels for 0%

commit v1 on v0

v1 whole, which is shorter than its diff:
```python
from functools import partial

import jax
import jax.numpy as jnp
from jax import lax
from jax.experimental import pallas as pl
from jax.experimental.pallas import tpu as pltpu
from jax.sharding import PartitionSpec as P

HEADS = 12
HEAD = 64
PAIR = 2 * HEAD
ROWS = 16
STEP = 10
EPSILON = 1e-05
LOG2E = 1.4426950408889634
LN2 = 0.6931471805599453
SCORE_SCALE = HEAD ** (-0.5) * LOG2E
MASKED = -1000000000.0 * LOG2E
LEAST, MOST = 2.0**-80, 2.0**100
CHUNK = 32
VMEM_BYTES = 64 * 1024 * 1024 - 128 * 1024

f32 = jnp.float32
bf16 = jnp.bfloat16

VMEM = pl.BlockSpec(memory_space=pltpu.VMEM)
SMEM = pl.BlockSpec(memory_space=pltpu.SMEM)
HBM = pl.BlockSpec(memory_space=pltpu.HBM)
ANY = pl.BlockSpec(memory_space=pl.ANY)


def product(left, right):
    return jnp.dot(left, right, preferred_element_type=f32)


def product_back(left, right):
    return lax.dot_general(left, right, (((1,), (1,)), ((), ())), preferred_element_type=f32)


def adamw(weight, moment, second, gradient):
    moment_new = 0.5 * moment + 0.5 * gradient
    second_new = 0.5 * second + 0.5 * gradient * gradient
    first_hat = moment_new / (1.0 - 0.5**STEP)
    second_hat = second_new / (1.0 - 0.5**STEP)
    weight_new = weight - 0.25 * (first_hat / (jnp.sqrt(second_hat) + 1e-08) + 0.01 * weight)
    return (moment_new, second_new, weight_new)


def shaped(shape, dtype):
    return jax.ShapeDtypeStruct(shape, dtype)


def buffers(*shapes, dtype=bf16):
    return [pltpu.VMEM(shape, dtype) for shape in shapes]


def lanes(shape):
    return lax.broadcasted_iota(jnp.int32, shape, len(shape) - 1)


def half_mask(which):
    return jnp.where(lanes((1, PAIR)) // HEAD == which, 1.0, 0.0).astype(bf16)


def row_chunks(rows, size=CHUNK):
    return [slice(at, at + size) for at in range(0, rows, size)]


def span_of(at, size):
    return pl.ds(pl.multiple_of(at * size, size), size)


def for_each(count, body):
    def step(at, carry):
        body(at)
        return carry

    lax.fori_loop(0, count, step, 0)


def make_copies(pairs, sems):
    return [pltpu.make_async_copy(src, dst, sems.at[n]) for n, (src, dst) in enumerate(pairs)]


def block_start(mask, block):
    return (lax.axis_index("seq") ^ mask) * block


def turned_rows(rows):
    pad = jnp.zeros((PAIR - rows.shape[0], rows.shape[1]), f32)
    return jnp.concatenate([rows, pad], axis=0).T


def call(kernel, name, args, in_specs, outs, scratch, flops, moved, powers=0):
    return pl.pallas_call(
        kernel,
        in_specs=in_specs,
        out_specs=[spec for spec, _, _ in outs],
        out_shape=[shaped(shape, dtype) for _, shape, dtype in outs],
        scratch_shapes=scratch,
        compiler_params=pltpu.CompilerParams(vmem_limit_bytes=VMEM_BYTES),
        cost_estimate=pl.CostEstimate(flops=flops, bytes_accessed=moved, transcendentals=powers),
        name=name,
    )(*args)


def both(rows):
    return rows[...].reshape(2 * rows.shape[1], rows.shape[2])


def project_keys(x, weights, k, kt):
    rows, width = x.shape[1:]
    keys = product(both(x), weights[:, 0:width])
    for block in range(2):
        for at in row_chunks(rows):
            k[block, at, :] = keys[block * rows + at.start : block * rows + at.stop].astype(bf16)
        kt[:, block * rows : (block + 1) * rows] = k[block].T


def project_values(x, weights, bias, v, vt):
    rows, width = x.shape[1:]
    values = product(both(x), weights[:, width : 2 * width])
    for block in range(2):
        for at in row_chunks(rows):
            part = values[block * rows + at.start : block * rows + at.stop]
            v[block, at, :] = (part + bias).astype(bf16)
        vt[:, block * rows : (block + 1) * rows] = v[block].T


def attend_fast(q, k, vt, e, o, l, has_prev, finish):
    rows, width = q.shape
    blocks = k.shape[0]
    ones = jnp.ones((ROWS, blocks * rows), bf16)

    def body(pair):
        span = span_of(pair, PAIR)
        for half in range(2):
            head = 2 * pair + half
            q_own = q[:, span] * half_mask(half)
            for block in range(blocks):
                scores = product_back(q_own, k[block, :, span])
                e[head, :, block * rows : (block + 1) * rows] = jnp.exp2(scores).astype(bf16)
            own = span_of(head, HEAD)
            out = product_back(jnp.concatenate([vt[own, :], ones], axis=0), e[head])
            row = pl.ds(head, 1)
            if has_prev:
                o[own, :] += out[:HEAD]
                l[row, :] += out[HEAD : HEAD + 1]
            else:
                o[own, :] = out[:HEAD]
                l[row, :] = out[HEAD : HEAD + 1]
        finish(pair)

    for_each(width // PAIR, body)


def attend_slow(q, k, vt, e, o, l, m, mb, col, has_prev, finish, starts, count):
    rows, width = q.shape
    blocks = k.shape[0]
    ones = jnp.ones((ROWS, blocks * rows), bf16)

    def body(pair):
        span = span_of(pair, PAIR)

        def one_half(half):
            head = 2 * pair + half

            def group(n):
                at = span_of(n, PAIR)
                q_own = q[at, span] * half_mask(half)
                parts = []
                for block in range(blocks):
                    scores = product_back(q_own, k[block, :, span])
                    position = starts[block] + lanes((PAIR, rows))
                    parts.append(jnp.where(position < count, scores, MASKED))
                top = jnp.max(parts[0], axis=1, keepdims=True)
                for part in parts[1:]:
                    top = jnp.maximum(top, jnp.max(part, axis=1, keepdims=True))
                for block in range(blocks):
                    e[head, at, block * rows : (block + 1) * rows] = jnp.exp2(
                        parts[block] - top
                    ).astype(bf16)
                col[at, :] = jnp.broadcast_to(top, (PAIR, PAIR))

            for_each(rows // PAIR, group)
            own = span_of(head, HEAD)
            row = pl.ds(head, 1)
            out = product_back(jnp.concatenate([vt[own, :], ones], axis=0), e[head])
            top = col[...].T[0:1, :]
            if has_prev:
                old = m[row, :]
                top_new = jnp.maximum(old, top)
                keep = jnp.exp2(old - top_new)
                add = jnp.exp2(top - top_new)
                o[own, :] = o[own, :] * keep + out[:HEAD] * add
                l[row, :] = l[row, :] * keep + out[HEAD : HEAD + 1] * add
                mb[row, :] = top
                m[row, :] = top_new
            else:
                o[own, :] = out[:HEAD]
                l[row, :] = out[HEAD : HEAD + 1]
                m[row, :] = top

        for_each(2, one_half)
        finish(pair)

    for_each(width // PAIR, body)


def attend(covered, q, k, vt, e, o, l, m, mb, col, has_prev, starts, count, finish, restore):
    @pl.when(covered)
    def _():
        attend_fast(q, k, vt, e, o, l, has_prev, finish)

    sums = l[...]
    safe = covered & (jnp.min(sums) > LEAST) & (jnp.max(sums) < MOST)

    @pl.when(jnp.logical_not(safe))
    def _():
        restore()
        attend_slow(q, k, vt, e, o, l, m, mb, col, has_prev, finish, starts, count)

    return safe


def near_kernel(
    count_ref,
    d_ref,
    b_ref,
    bias_ref,
    x_hbm,
    wk_hbm,
    a_hbm,
    sb_hbm,
    wq_hbm,
    wv_hbm,
    x_one_hbm,
    fast_ref,
    l,
    m,
    e_hbm,
    o_hbm,
    q_hbm,
    qt_hbm,
    v_hbm,
    kt_hbm,
    w_all_hbm,
    bt_hbm,
    x,
    a,
    sb,
    w,
    scaled,
    e,
    o,
    q,
    qt,
    k,
    v,
    kt,
    vt,
    w_all,
    bt,
    col,
    sems_in,
    sems_out,
    sems_e,
):
    rows, width = x.shape[1:]
    come = make_copies(
        (
            (x_hbm, x.at[0]),
            (a_hbm, a),
            (sb_hbm, sb),
            (wq_hbm, w.at[0]),
            (wk_hbm, w_all.at[:, pl.ds(width, width)]),
            (wv_hbm, w.at[1]),
            (x_one_hbm, x.at[1]),
        ),
        sems_in,
    )
    for n in (0, 6, 4, 1, 2, 3, 5):
        come[n].start()
    leave = make_copies(
        ((q, q_hbm), (qt, qt_hbm), (v, v_hbm), (kt, kt_hbm), (w_all, w_all_hbm), (bt, bt_hbm), (o, o_hbm)),
        sems_out,
    )
    l[...] = jnp.ones_like(l)
    m[...] = jnp.zeros_like(m)

    def folded(n, w):
        for at in row_chunks(width):
            scaled[at, :] = (a[at, :].astype(f32) * d_ref[n : n + 1, :]).astype(bf16)
        adapter = product(scaled[...], sb[...])
        for at in row_chunks(width):
            out = w[at, :].astype(f32) + adapter[at] * b_ref[n : n + 1, :]
            w_all[at, spans[2 * n]] = out.astype(bf16)

    kv = w_all.at[:, pl.ds(width, 2 * width)]
    for n in (0, 6, 4):
        come[n].wait()
    project_keys(x, kv, k, kt)
    leave[3].start()
    for n in (1, 2, 3, 5):
        come[n].wait()

    def folded(n):
        row = pl.ds(n, 1)
        for at in row_chunks(width):
            scaled[at, :] = (a[at, :].astype(f32) * d_ref[row, :]).astype(bf16)
        adapter = product(scaled[...], sb[...])
        span = span_of(2 * n, width)
        for at in row_chunks(width):
            out = w[n, at, :].astype(f32) + adapter[at] * b_ref[row, :]
            w_all[at, span] = out.astype(bf16)

    for_each(2, folded)
    leave[4].start()
    queries = product(x[0], w_all[:, 0:width])
    for at in row_chunks(rows):
        q[at, :] = ((queries[at] + bias_ref[0:1, :]) * SCORE_SCALE).astype(bf16)
    leave[0].start()
    qt[...] = q[...].T
    leave[1].start()
    bt[...] = sb[...].T
    leave[5].start()
    project_values(x, kv, bias_ref[1:2, :], v, vt)
    leave[2].start()
    count = count_ref[0]
    starts = (block_start(0, rows), block_start(1, rows))
    covered = jnp.maximum(*starts) + rows <= count

    def copy_e(pair):
        heads = pl.ds(2 * pair, 2)
        return pltpu.make_async_copy(e.at[heads], e_hbm.at[heads], sems_e.at[pair])

    def restore():
        @pl.when(covered)
        def _():
            for pair in range(width // PAIR):
                copy_e(pair).wait()

    safe = attend(
        covered, q, k, vt, e, o, l, m, m, col, False, starts, count, lambda pair: copy_e(pair).start(), restore
    )
    fast_ref[0] = jnp.where(safe, 1, 0)
    leave[6].start()
    for copy in leave:
        copy.wait()
    for pair in range(width // PAIR):
        copy_e(pair).wait()


def near(lengths, d, b, biases, x, w_key, shared_a, shared_b, w_query, w_value, x_one):
    rows, width = x.shape
    rank = shared_a.shape[1]
    low, square, expo = (rows, width), (width, width), (HEADS, rows, 2 * rows)
    turned = (width, 2 * rows)
    return call(
        near_kernel,
        "near",
        (lengths, d, b, biases, x, w_key, shared_a, shared_b, w_query, w_value, x_one),
        [SMEM, VMEM, VMEM, VMEM] + [HBM] * 6 + [ANY],
        [
            (SMEM, (1,), jnp.int32),
            (VMEM, (ROWS, rows), f32),
            (VMEM, (ROWS, rows), f32),
            (HBM, expo, bf16),
            (HBM, (width, rows), f32),
            (HBM, low, bf16),
            (HBM, (width, rows), bf16),
            (HBM, (2,) + low, bf16),
            (HBM, turned, bf16),
            (HBM, (width, 3 * width), bf16),
            (HBM, (width, rank), bf16),
        ],
        buffers((2,) + low, (width, rank), (rank, width), (2,) + square, (width, rank), expo)
        + buffers((width, rows), dtype=f32)
        + buffers(low, (width, rows), (2,) + low, (2,) + low, turned, turned)
        + buffers((width, 3 * width), (width, rank))
        + buffers((rows, PAIR), dtype=f32)
        + [
            pltpu.SemaphoreType.DMA((7,)),
            pltpu.SemaphoreType.DMA((7,)),
            pltpu.SemaphoreType.DMA((width // PAIR,)),
        ],
        32 * rows * rows * width + 10 * rows * width * width + 4 * width * rank * width,
        40 * 1024 * 1024,
        2 * HEADS * rows * rows,
    )


def attend_back(
    go, got, qt, less, factor, v, kt, e, gqt, gvts, gkvs, scores, ready, done
):
    rows, width = go.shape
    blocks = len(v)
    lane = lanes((rows, PAIR))

    def body(pair):
        span = span_of(pair, PAIR)
        ready(pair)
        g_values, g_keys = [], []
        for half in range(2):
            head = 2 * pair + half
            left = jnp.concatenate([go[:, span] * half_mask(half), less[...]], axis=1)
            picks = jnp.where(lane // 2 == head, 1.0, 0.0).astype(bf16)
            towards = [
                product_back(left, jnp.concatenate([v[block][:, span], picks], axis=1))
                for block in range(blocks)
            ]
            own = jnp.sum(jnp.where(lane == head, factor[...], 0.0), axis=1, keepdims=True)
            own = jnp.broadcast_to(own, (rows, PAIR)).astype(bf16)
            own = jnp.concatenate([own] * (rows // PAIR), axis=1)
            for block in range(blocks):
                here = slice(block * rows, (block + 1) * rows)
                for at in row_chunks(rows):
                    weights = e[head, at, here] * own[at]
                    e[head, at, here] = weights
                    scores[half, at, here] = weights * towards[block][at].astype(bf16)
            span_own = span_of(head, HEAD)
            g_values.append(product(got[span_own, :], e[head]).astype(bf16))
            g_keys.append((product(qt[span_own, :], scores[half]) * LN2).astype(bf16))
            gqt[span_own, :] += product_back(kt[span_own, :], scores[half])
        g_values = jnp.concatenate(g_values, axis=0)
        g_keys = jnp.concatenate(g_keys, axis=0)
        value_span = pl.ds(pl.multiple_of(width + pair * PAIR, PAIR), PAIR)
        for block in range(blocks):
            here = slice(block * rows, (block + 1) * rows)
            gvts[block][span, :] = g_values[:, here]
            gkvs[block][:, span] = g_keys[:, here].T
            gkvs[block][:, value_span] = g_values[:, here].T
        done(pair)

    for_each(width // PAIR, body)


def norm_parts(values):
    width = values.shape[1]
    centred = values - jnp.sum(values, axis=1, keepdims=True) * (1.0 / width)
    variance = jnp.sum(centred * centred, axis=1, keepdims=True) * (1.0 / width)
    scale = lax.rsqrt(variance + EPSILON)
    return centred * scale, scale


def norm_back(grad, hat, scale):
    width = grad.shape[1]
    mean = jnp.sum(grad, axis=1, keepdims=True) * (1.0 / width)
    along = jnp.sum(grad * hat, axis=1, keepdims=True) * (1.0 / width)
    return scale * (grad - mean - hat * along)


def gelu_pair(x):
    phi = 0.5 + 0.5 * lax.erf(x * 0.7071067811865476)
    bell = jnp.exp2(x * x * (-0.5 * LOG2E))
    return x * phi, phi + x * bell * 0.3989422804014327


def middle(
    count,
    o,
    invt,
    x,
    cot,
    go,
    got,
    acc_ref,
    lesst,
    hat_ref,
    low_ref,
    pool,
    scale_ref,
    bias_ref,
    bias_up_ref,
    gain_ref,
    w_out,
    w_up,
    w_down,
    waits,
    sends,
):
    rows, width = x.shape
    hidden = w_up.shape[1]
    chunk = 512
    slabs = pool.shape[0] // 2
    wide = pool.shape[2]

    def slab_of(start):
        return start // wide, slice(start % wide, start % wide + chunk)


    for head in range(HEADS):
        own = slice(head * HEAD, (head + 1) * HEAD)
        o[own, :] = o[own, :] * invt[head : head + 1, :]
    low_ref[...] = o[...].astype(bf16).T
    waits[0]()
    attn = product(low_ref[...], w_out[...])
    for at in row_chunks(rows):
        hat, scale = norm_parts(x[at, :].astype(f32) + attn[at] + bias_ref[2:3, :])
        scale_ref[at, :] = jnp.broadcast_to(scale, (CHUNK, PAIR))
        hat_ref[at, :] = hat.astype(bf16)
        normed = hat * gain_ref[0:1, :] + bias_ref[4:5, :]
        low_ref[at, :] = normed.astype(bf16)
        acc_ref[at, :] = normed + bias_ref[3:4, :]
    waits[1]()

    for start in range(0, hidden, chunk):
        span = slice(start, start + chunk)
        slab, here = slab_of(start)
        pre = product(low_ref[...], w_up[:, span])
        for at in row_chunks(rows):
            bent, slope = gelu_pair(pre[at] + bias_up_ref[:, span])
            pool[slab, at, here] = bent.astype(bf16)
            pool[slabs + slab, at, here] = slope.astype(bf16)
    waits[2]()

    def slabs_of_pool():
        return jnp.concatenate([pool[slab] for slab in range(slabs)], axis=1)

    ffn = product(slabs_of_pool(), w_down[...])
    waits[3]()
    first = block_start(0, rows)
    for at in row_chunks(rows):
        hat, scale = norm_parts(acc_ref[at, :] + ffn[at])
        position = first + at.start + lax.broadcasted_iota(jnp.int32, (CHUNK, 1), 0)
        valid = jnp.where(position < count, 1.0, 0.0)
        grad = cot[at, :].astype(f32) * gain_ref[1:2, :]
        cot[at, :] = ((hat * gain_ref[1:2, :] + bias_ref[5:6, :]) * valid).astype(bf16)
        g_two = norm_back(grad, hat, scale * valid)
        low_ref[at, :] = g_two.astype(bf16)
        acc_ref[at, :] = g_two
    sends[0]()

    for start in range(0, hidden, chunk):
        slab, here = slab_of(start)
        g_hidden = product_back(low_ref[...], w_down[start : start + chunk, :])
        for at in row_chunks(rows):
            g_pre = g_hidden[at] * pool[slabs + slab, at, here].astype(f32)
            pool[slab, at, here] = g_pre.astype(bf16)
    g_up = product_back(slabs_of_pool(), w_up[...])
    for at in row_chunks(rows):
        grad = (acc_ref[at, :] + g_up[at]) * gain_ref[0:1, :]
        out = norm_back(grad, hat_ref[at, :].astype(f32), scale_ref[at, 0:1])
        acc_ref[at, :] = out
        low_ref[at, :] = out.astype(bf16)
    sends[1]()
    grad_out = product_back(low_ref[...], w_out[...])
    for at in row_chunks(rows):
        go[at, :] = grad_out[at].astype(bf16)
    got[...] = go[...].T
    lesst[...] = jnp.zeros_like(lesst)
    for head in range(HEADS):
        own = slice(head * HEAD, (head + 1) * HEAD)
        delta = jnp.sum(got[own, :].astype(f32) * o[own, :], axis=0, keepdims=True)
        high = delta.astype(bf16).astype(f32)
        lesst[2 * head : 2 * head + 1, :] = -high
        lesst[2 * head + 1 : 2 * head + 2, :] = high - delta


def far_kernel(
    count_ref,
    fast_ref,
    bias_ref,
    bias_up_ref,
    gain_ref,
    d_ref,
    b_ref,
    l_prev,
    m_prev,
    w_all_hbm,
    x_two_hbm,
    x_three_hbm,
    q_hbm,
    o_hbm,
    w_out_hbm,
    w_up_hbm,
    w_down_hbm,
    x_hbm,
    cot_hbm,
    qt_hbm,
    x_one_hbm,
    v_near_hbm,
    kt_near_hbm,
    e_near_hbm,
    a_hbm,
    bt_hbm,
    total_ref,
    act_hbm,
    rest_hbm,
    two_hbm,
    three_hbm,
    one_hbm,
    w_all,
    x_far,
    q,
    o,
    w_out,
    w_up,
    w_down,
    x,
    cot,
    qt,
    g_one,
    got,
    kv,
    turned,
    e,
    pool,
    gkv,
    scores,
    l,
    m,
    mb,
    lesst,
    less,
    factors,
    scale_ref,
    hat_ref,
    sems_in,
    sems_e,
    sems_late,
    sems_out,
):
    rows, width = x.shape
    pairs = width // PAIR
    go, low_ref = q, x_far.at[1]
    come = make_copies(
        (
            (w_all_hbm, w_all),
            (x_two_hbm, x_far.at[0]),
            (x_three_hbm, x_far.at[1]),
            (q_hbm, q),
            (o_hbm, o),
            (w_out_hbm, w_out),
            (x_hbm, x),
            (w_up_hbm, w_up),
            (w_down_hbm, w_down),
            (cot_hbm, cot),
            (qt_hbm, qt),
        ),
        sems_in,
    )
    for copy in come[:3]:
        copy.start()
    v, k = kv.at[pl.ds(0, 2)], kv.at[pl.ds(2, 2)]
    kt, vt = turned.at[0], turned.at[1]
    x_all = w_down.at[pl.ds(0, 4 * rows)]
    a = w_up.at[:, pl.ds(0, 2 * rows)]
    gvt_all = w_up.at[:, pl.ds(2 * rows, 4 * rows)]
    late = make_copies(
        (
            (v_near_hbm, k),
            (kt_near_hbm, vt),
            (x_hbm, x_all.at[pl.ds(0, rows)]),
            (x_one_hbm, x_all.at[pl.ds(rows, rows)]),
            (x_two_hbm, x_all.at[pl.ds(2 * rows, rows)]),
            (x_three_hbm, x_all.at[pl.ds(3 * rows, rows)]),
            (a_hbm, a),
            (bt_hbm, kt),
        ),
        sems_late,
    )
    leave = make_copies(
        (
            (cot, act_hbm),
            (x_far.at[0], two_hbm),
            (x_far.at[1], three_hbm),
            (g_one, rest_hbm),
            (x_far.at[1], one_hbm),
        ),
        sems_out,
    )

    def copy_e(pair):
        heads = pl.ds(2 * pair, 2)
        return pltpu.make_async_copy(e_near_hbm.at[heads], e.at[heads], sems_e.at[pair])

    l[...] = l_prev[...]
    m[...] = m_prev[...]
    mb[...] = jnp.zeros_like(mb)
    wkv = w_all.at[:, pl.ds(width, 2 * width)]
    for copy in come[:3]:
        copy.wait()
    for copy in come[3:]:
        copy.start()
    project_keys(x_far, wkv, k, kt)
    project_values(x_far, wkv, bias_ref[1:2, :], v, vt)
    count = count_ref[0]
    starts = (block_start(2, rows), block_start(3, rows))
    covered = (jnp.maximum(*starts) + rows <= count) & (fast_ref[0] == 1)
    come[3].wait()
    come[4].wait()

    def restore():
        l[...] = l_prev[...]
        again = pltpu.make_async_copy(o_hbm, o, sems_in.at[4])
        again.start()
        again.wait()

    col = factors.at[0]
    attend(covered, q, k, vt, e, o, l, m, mb, col, True, starts, count, lambda pair: None, restore)
    for copy in late[:2]:
        copy.start()

    invt = 1.0 / l[...]
    factors[0] = turned_rows(invt * jnp.exp2(mb[...] - m[...]))
    factors[1] = turned_rows(invt * jnp.exp2(m_prev[...] - m[...]))

    def waits(*which):
        def wait():
            for n in which:
                come[n].wait()

        return wait

    def fetch_late():
        for copy in late[2:7]:
            copy.start()

    middle(
        count,
        o,
        invt,
        x,
        cot,
        go,
        got,
        g_one,
        lesst,
        hat_ref,
        low_ref,
        pool,
        scale_ref,
        bias_ref,
        bias_up_ref,
        gain_ref,
        w_out,
        w_up,
        w_down,
        (waits(5, 6), waits(7), waits(8), waits(9, 10)),
        (leave[0].start, fetch_late),
    )
    less[...] = lesst[...].T.astype(bf16)
    o[...] = jnp.zeros_like(o)

    def one_chip(chip):
        own = chip == 1

        @pl.when(own)
        def _():
            late[0].wait()
            late[1].wait()

        def ready(pair):
            @pl.when(own)
            def _():
                copy_e(pair).wait()

        def done(pair):
            @pl.when(jnp.logical_not(own))
            def _():
                copy_e(pair).start()

        attend_back(
            go,
            got,
            qt,
            less,
            factors.at[chip],
            [kv.at[2 * chip + block] for block in range(2)],
            turned.at[chip],
            e,
            o,
            [gvt_all.at[:, span_of(2 - 2 * chip + block, rows)] for block in range(2)],
            (gkv.at[0], gkv.at[1]),
            scores,
            ready,
            done,
        )

        @pl.when(own)
        def _():
            leave[1].wait()
            leave[2].wait()

        out = product_back(both(gkv), wkv[...])
        for block in range(2):
            for at in row_chunks(rows):
                part = out[block * rows + at.start : block * rows + at.stop]
                x_far[block, at, :] = part.astype(bf16)

        @pl.when(own)
        def _():
            leave[4].start()

        @pl.when(jnp.logical_not(own))
        def _():
            leave[1].start()
            leave[2].start()
            late[7].start()

    for_each(2, one_chip)
    for at in row_chunks(width):
        got[at, :] = (o[at, :] * HEAD ** (-0.5)).astype(bf16)
    go[...] = got[...].T
    out = product_back(go[...], w_all[:, 0:width])
    for at in row_chunks(rows):
        g_one[at, :] += out[at] + x_far[0, at, :].astype(f32)
    leave[3].start()
    for copy in late[2:]:
        copy.wait()
    bt = kt
    rank = a.shape[1]
    total_ref[...] = jnp.zeros_like(total_ref)
    eye = lax.broadcasted_iota(jnp.int32, (PAIR, PAIR), 0) == lanes((PAIR, PAIR))
    for n in range(2):
        if n == 0:
            outer = product(got[...], x_all[0:rows, :])
        else:
            outer = product(gvt_all[...], x_all[...])
        mixed = product(outer.astype(bf16), a[...])
        for_d = jnp.zeros((1, rank), f32)
        for at in row_chunks(width, PAIR):
            part = mixed[at] * bt[at, :].astype(f32)
            column = jnp.sum(jnp.where(eye, b_ref[n : n + 1, at], 0.0), axis=1, keepdims=True)
            for_d = for_d + jnp.sum(part * column, axis=0, keepdims=True)
            sums = jnp.sum(part * d_ref[n : n + 1, :], axis=1, keepdims=True)
            total_ref[2 + n : 3 + n, at] = jnp.sum(jnp.where(eye, sums, 0.0), axis=0, keepdims=True)
        total_ref[n : n + 1, :] = for_d
    for copy in (leave[0], leave[3], leave[4]):
        copy.wait()


def far(small, large):
    w_all, x_two, x_three, q, o, w_out, w_up, w_down = large[:8]
    a = large[-2]
    rows, width = x_two.shape
    hidden = w_up.shape[1]
    rank = a.shape[1]
    low, square, expo = (rows, width), (width, width), (HEADS, rows, 2 * rows)
    turned, row, stat = (width, 2 * rows), (ROWS, rows), (rows, PAIR)
    flat = (width, rows)
    places = [HBM, ANY, ANY] + [HBM] * (len(large) - 3)
    places[11] = ANY
    return call(
        far_kernel,
        "far",
        (*small, *large),
        [SMEM] * 2 + [VMEM] * (len(small) - 2) + places,
        [
            (VMEM, (4, rank), f32),
            (HBM, low, bf16),
            (HBM, low, f32),
            (HBM, low, bf16),
            (HBM, low, bf16),
            (HBM, low, bf16),
        ],
        buffers((width, 3 * width), (2,) + low, low)
        + buffers(flat, dtype=f32)
        + buffers(square, (width, hidden), (hidden, width), low, low, flat)
        + buffers(low, dtype=f32)
        + buffers(flat, (4,) + low, (2,) + turned, expo)
        + buffers((2 * hidden // (2 * rows), rows, 2 * rows))
        + buffers((2, rows, 2 * width), (2, rows, 2 * rows))
        + buffers(row, row, row, (PAIR, rows), dtype=f32)
        + buffers(stat)
        + buffers((2,) + stat, stat, dtype=f32)
        + buffers(low)
        + [
            pltpu.SemaphoreType.DMA((11,)),
            pltpu.SemaphoreType.DMA((width // PAIR,)),
            pltpu.SemaphoreType.DMA((8,)),
            pltpu.SemaphoreType.DMA((5,)),
        ],
        160 * rows * rows * width + 30 * rows * width * width + 8 * rows * width * hidden,
        60 * 1024 * 1024,
        2 * HEADS * rows * rows + 2 * rows * hidden,
    )


def tree_sum(terms):
    while len(terms) > 1:
        terms = [terms[n] + terms[n + 1] for n in range(0, len(terms), 2)]
    return terms[0]


def step_kernel(count, *refs):
    totals = tree_sum([ref[...] for ref in refs[:count]])
    weights = refs[count : count + 6]
    outs = refs[count + 6 :]
    for n in range(2):
        weight, moment, second = weights[3 * n : 3 * n + 3]
        grad = totals[2 * n : 2 * n + 2, : weight.shape[1]]
        moment_new, second_new, weight_new = adamw(weight[...], moment[...], second[...], grad)
        outs[2 * n][...] = moment_new
        outs[2 * n + 1][...] = second_new
        outs[4 + n][...] = weight_new
        outs[6 + n][...] = weight_new.astype(bf16)


def step(terms, weights):
    d, b = weights[0].shape, weights[3].shape
    shapes = [(s, f32) for s in (d, d, b, b, d, b)] + [(d, bf16), (b, bf16)]
    return pl.pallas_call(
        partial(step_kernel, len(terms)),
        in_specs=[VMEM] * (len(terms) + 6),
        out_specs=[VMEM] * 8,
        out_shape=[shaped(*one) for one in shapes],
        name="step",
    )(*terms, *weights)


def swap(value, axis, size, mask):
    return lax.ppermute(value, axis, [(i, i ^ mask) for i in range(size)])


def partners(value, axis, size, stride):
    radix = min(4, size // stride)
    return [value] + [swap(value, axis, size, n * stride) for n in range(1, radix)]


def per_device(
    seq_size,
    dp_size,
    tokens,
    lengths,
    cotangent,
    w_query,
    w_key,
    w_value,
    w_out,
    w_up,
    w_down,
    shared_a,
    shared_b,
    vec_biases,
    bias_up,
    norm_gains,
    scale_d,
    scale_b,
    mom_d,
    sec_d,
    mom_b,
    sec_b,
):
    _, local_len, width = tokens.shape
    x = tokens.reshape(local_len, width)
    x_one = swap(x, "seq", seq_size, 1)
    x_two = swap(x, "seq", seq_size, 2)
    fast, l, m, e_near, o, q, qt, v_near, kt_near, w_all, b_turned = near(
        lengths, scale_d, scale_b, vec_biases, x, w_key, shared_a, shared_b, w_query, w_value, x_one
    )
    x_two, o = lax.optimization_barrier((x_two, o))
    x_three = swap(x_two, "seq", seq_size, 1)
    totals, activations, rest, two, three, one = far(
        (
            lengths,
            fast,
            vec_biases,
            bias_up.reshape(1, -1),
            norm_gains,
            scale_d,
            scale_b,
            l,
            m,
        ),
        (
            w_all,
            x_two,
            x_three,
            q,
            o,
            w_out,
            w_up,
            w_down,
            x,
            cotangent.reshape(local_len, width),
            qt,
            x_one,
            v_near,
            kt_near,
            e_near,
            shared_a,
            b_turned,
        ),
    )
    from_three = swap(three, "seq", seq_size, 1)
    joined = (two.astype(f32) + from_three.astype(f32)).astype(bf16)
    terms = partners(totals, "seq", seq_size, 1)
    joined, *terms = lax.optimization_barrier((joined, *terms))
    from_two = swap(joined, "seq", seq_size, 2)
    from_one = swap(one, "seq", seq_size, 1)
    stride = 1
    while stride < dp_size:
        terms = partners(tree_sum(terms), "dp", dp_size, stride)
        stride *= len(terms)
    moment_d, second_d, moment_b, second_b, new_d, new_b, copy_d, copy_b = step(
        terms, (scale_d, mom_d, sec_d, scale_b, mom_b, sec_b)
    )
    grad_inputs = rest + from_one.astype(f32) + from_two.astype(f32)
    return (
        activations.reshape(tokens.shape),
        grad_inputs.reshape(tokens.shape),
        moment_d,
        second_d,
        moment_b,
        second_b,
        new_d,
        new_b,
        copy_d,
        copy_b,
    )


def solution(mesh):
    rows = P("dp", "seq", None)
    return jax.shard_map(
        partial(per_device, mesh.shape["seq"], mesh.shape["dp"]),
        mesh=mesh,
        in_specs=(rows, P("dp"), rows) + (P(),) * 17,
        out_specs=(rows, rows) + (P(),) * 8,
        check_vma=False,
    )
```

time: 324 us -> 125 us (0.39)
  matrix products: 191 us -> 0 us
  Pallas kernels: 0 us -> 92.9 us
  blocking collectives: 40.1 us -> 0 us
  other arithmetic: 34 us -> 3.56 us
  local copies, waits for them, and re-layouts: 21.1 us -> 0.61 us
  between operations: 15.5 us -> 1.38 us
  starting transfers between devices: 0.38 us -> 13.1 us
  waiting for transfers between devices: 18.9 us -> 13.2 us
    dot_general x23 -> x0, matrix products: 191 us -> none  [the longest x9 33.3 us: product(): return jnp.dot(left, right, preferred_element_type=jnp.float32)]
    pallas_call x0 -> x3, Pallas kernels: none -> 92.9 us  [the longest x2 91.4 us: call(): pl.pallas_call(kernel, in_specs=in_specs, out_specs=[spec for spec, _, _...]
    psum x1 -> x0, blocking collectives: 40.1 us -> none  [per_device(): total_d, total_b = lax.psum((total_d, total_b), ('dp', 'seq'))]
    reduce_sum x8 -> x0, other arithmetic: 32.6 us -> none  [the longest x1 22 us: per_sequence(): total_new = total * rescale + jnp.sum(weights, axis=-1)]
    all_gather x2 -> x0, waiting for transfers between devices: 18.9 us -> none  [the longest x1 18.8 us: per_device(): lax.all_gather(keys, 'seq', axis=1, tiled=True)]
    ppermute x0 -> x13, waiting for transfers between devices: none -> 13.2 us  [swap(): return lax.ppermute(value, axis, [(i, i ^ mask) for i in range(size)])]
    ppermute x0 -> x13, starting transfers between devices: none -> 13.1 us  [swap(): return lax.ppermute(value, axis, [(i, i ^ mask) for i in range(size)])]
    all_gather x2 -> x0, local copies, waits for them, and re-layouts: 9.46 us -> none  [the longest x1 4.74 us: per_device(): lax.all_gather(values, 'seq', axis=1, tiled=True)]
  transfers between devices with their start and end apart: 4 -> 13, of which waited for: 1 -> 7; matrix products, arithmetic and copies ran while one was open for 42% -> 2% of each run, Pallas kernels for 0% -> 16%
where the time goes in v1:
time: 125 us
  Pallas kernels  92.9 us (74%)
  waiting for transfers between devices  13.2 us (11%)
  starting transfers between devices  13.1 us (10%)
  other arithmetic  3.56 us (3%)
  between operations  1.38 us (1%)
    pallas_call x2, Pallas kernels, call(): pl.pallas_call(kernel, in_specs=in_specs, out_specs=[spec for spec, _, _...  91.4 us
    ppermute x13, waiting for transfers between devices, swap(): return lax.ppermute(value, axis, [(i, i ^ mask) for i in range(size)])  13.2 us
    ppermute x13, starting transfers between devices, swap(): return lax.ppermute(value, axis, [(i, i ^ mask) for i in range(size)])  13.1 us
  transfers between devices with their start and end apart: 13, of which 7 were waited for; matrix products, arithmetic and copies ran while one was open for 2% of the time, Pallas kernels for 16%

profile of v1, /device:TPU:0, one launch (start us, length us, event | category | flops | bytes accessed | tf_op | source)
XLA Modules:
  0.0 124.7 jit_solution(2019073382679122992)
XLA Ops:
  0.6 0.5 collective-permute-start
  1.2 2.6 %collective-permute-start.1 = (bf16[512,768]{1,0:T(8,128)(2,1)}, bf16[512,768]{1,0:T(8,128)(2,1)}, u32[]{:S(2)}, u32[]{:S(2)}) collective-permute-start(bf16[512,768]{1,0:T(8,128)(2,1)} %bitcast.7), channel_id=1, source_target_pairs={{0,2},{1,3},{2,0},{3,1},{4,6},{5,7},{6,4},{7,5},{8,10},{9,11},{10,... | collective-permute-start | bytes 2359304 | tf_op jit(solution)/shard_map/ppermute | solution.py:915
  4.4 0.0 collective-permute-done.x_one_hbm
  4.4 19.0 %near.1 = (s32[1]{0:T(128)}, f32[16,512]{1,0:T(8,128)}, f32[16,512]{1,0:T(8,128)}, bf16[12,512,1024]{2,1,0:T(8,128)(2,1)}, f32[768,512]{1,0:T(8,128)}, /*index=5...) custom-call(s32[1]{0:T(128)S(6)} %copy.30.count_ref, ...), custom_call_target="tpu_custom_call" | custom-call | flops 11878268928 | bytes 41943040 | tf_op jit(solution)/shard_map/near/pallas_call | solution.py:96
  23.4 0.0 collective-permute-done.1.x_two_hbm
  23.4 0.2 collective-permute-start.2
  23.7 2.5 %collective-permute-done.2.x_three_hbm = bf16[512,768]{1,0:T(8,128)(2,1)} collective-permute-done((bf16[512,768]{1,0:T(8,128)(2,1)}, bf16[512,768]{1,0:T(8,128)(2,1)}, u32[]{:S(2)}, u32[]{:S(2)}) %collective-permute-start.2) | collective-permute-done | bytes 786464 | tf_op jit(solution)/shard_map/ppermute | solution.py:915
  26.1 72.4 %far.1 = (f32[4,1024]{1,0:T(4,128)}, bf16[512,768]{1,0:T(8,128)(2,1)}, f32[512,768]{1,0:T(8,128)}, bf16[512,768]{1,0:T(8,128)(2,1)}, bf16[512,768]{1,0:T(8,128)(2,1)}, /*index=5*/bf16[512,768]{1,0:T(8,128)(2,1)}) custom-call(s32[1]{0:T(128)S(6)} %copy.30.count_ref, s32[1]{0:T(128)} %get-tuple-element.42.fast_ref, f32[6,768]{1,0:T(8,128)} %bias_ref.3, ...), custom_call_target="tpu_custom_call" | custom-call | flops 50935627776 | bytes 62914560 | tf_op jit(solution)/shard_map/far/pallas_call | solution.py:96
  98.6 0.0 copy-start.2
  98.6 0.0 copy-start
  98.6 0.2 collective-permute-start.4
  98.8 1.8 %collective-permute-start.7 = (f32[4,1024]{1,0:T(4,128)}, f32[4,1024]{1,0:T(4,128)S(1)}, u32[]{:S(2)}, u32[]{:S(2)}) collective-permute-start(f32[4,1024]{1,0:T(4,128)} %get-tuple-element.62), channel_id=1, source_target_pairs={{0,3},{1,2},{2,1},{3,0},{4,7},{5,6},{6,5},{7,4},{8,11},{9,10},{10,... | collective-permute-start | bytes 49160 | tf_op jit(solution)/shard_map/ppermute | solution.py:915
  100.6 0.2 collective-permute-start.6
  100.8 0.0 collective-permute-start.5
  100.8 0.5 collective-permute-start.3
  101.3 0.0 collective-permute-done.4
  101.3 2.2 %add_convert_fusion = bf16[512,768]{1,0:T(8,128)(2,1)} fusion(bf16[512,768]{1,0:T(8,128)(2,1)S(1)} %collective-permute-done.4, bf16[512,768]{1,0:T(8,128)(2,1)} %get-tuple-element.58), kind=kLoop, calls=%fused_computation.1 | loop fusion | flops 1572864 | bytes 2359296 | tf_op jit(solution)/shard_map/convert_element_type | solution.py:989
  103.5 0.0 collective-permute-done.7
  103.5 1.1 collective-permute-done.6
  104.6 0.0 collective-permute-done.5
  104.6 0.9 collective-permute-start.8
  105.4 0.0 copy-done.2
  105.5 2.6 %collective-permute-start.11 = (f32[4,1024]{1,0:T(4,128)S(1)}, f32[4,1024]{1,0:T(4,128)S(1)}, u32[]{:S(2)}, u32[]{:S(2)}) collective-permute-start(f32[4,1024]{1,0:T(4,128)S(1)} %add_add_fusion.1), channel_id=1, source_target_pairs={{0,12},{4,8},{8,4},{12,0},{16,28},{20,24},{24,20},{28,16},{1,13},{... | collective-permute-start | bytes 49160 | tf_op jit(solution)/shard_map/ppermute | solution.py:915
  108.0 0.4 collective-permute-start.10
  108.5 0.5 collective-permute-start.9
  109.0 1.3 %collective-permute-done.11 = f32[4,1024]{1,0:T(4,128)S(1)} collective-permute-done((f32[4,1024]{1,0:T(4,128)S(1)}, f32[4,1024]{1,0:T(4,128)S(1)}, u32[]{:S(2)}, u32[]{:S(2)}) %collective-permute-start.11) | collective-permute-done | bytes 16416 | tf_op jit(solution)/shard_map/ppermute | solution.py:915
  110.3 1.5 %collective-permute-done.10 = f32[4,1024]{1,0:T(4,128)S(1)} collective-permute-done((f32[4,1024]{1,0:T(4,128)S(1)}, f32[4,1024]{1,0:T(4,128)S(1)}, u32[]{:S(2)}, u32[]{:S(2)}) %collective-permute-start.10) | collective-permute-done | bytes 16416 | tf_op jit(solution)/shard_map/ppermute | solution.py:915
  111.8 0.4 collective-permute-done.9
  112.2 0.0 copy-start.1
  112.3 2.6 %collective-permute-start.12 = (f32[4,1024]{1,0:T(4,128)S(1)}, f32[4,1024]{1,0:T(4,128)S(1)}, u32[]{:S(2)}, u32[]{:S(2)}) collective-permute-start(f32[4,1024]{1,0:T(4,128)S(1)} %add_add_fusion.refs_0_), channel_id=1, source_target_pairs={{0,16},{4,20},{8,24},{12,28},{16,0},{20,4},{24,8},{28,12},{1,17},{... | collective-permute-start | bytes 49160 | tf_op jit(solution)/shard_map/ppermute | solution.py:915
  114.9 2.1 %collective-permute-done.12.refs_1_ = f32[4,1024]{1,0:T(4,128)S(1)} collective-permute-done((f32[4,1024]{1,0:T(4,128)S(1)}, f32[4,1024]{1,0:T(4,128)S(1)}, u32[]{:S(2)}, u32[]{:S(2)}) %collective-permute-start.12) | collective-permute-done | bytes 16416 | tf_op jit(solution)/shard_map/ppermute | solution.py:915
  117.0 0.0 copy-done.1
  117.0 0.0 copy-start.3
  117.0 0.6 copy-done.3
  117.6 1.4 %step.1 = (f32[2,1024]{1,0:T(2,128)}, f32[2,1024]{1,0:T(2,128)}, f32[2,768]{1,0:T(2,128)}, f32[2,768]{1,0:T(2,128)}, f32[2,1024]{1,0:T(2,128)}, /*index=5*/f32[2...) custom-call(f32[4,1024]{1,0:T(4,128)} %copy-done.1, f32[4,1024]{1,0:T(4,128)} %copy-done.3, f32[2,1024]{1,0:T(2,128)} %refs_2_.1, ...), custom_call_target="tpu_custom_call" | custom-call | tf_op jit(solution)/shard_map/step/pallas_call | solution.py:905
  119.0 0.0 collective-permute-done.3
  119.0 4.4 %collective-permute-done.8 = bf16[512,768]{1,0:T(8,128)(2,1)S(1)} collective-permute-done((bf16[512,768]{1,0:T(8,128)(2,1)}, bf16[512,768]{1,0:T(8,128)(2,1)S(1)}, u32[]{:S(2)}, u32[]{:S(2)}) %collective-permute-start.8) | collective-permute-done | bytes 786464 | tf_op jit(solution)/shard_map/ppermute | solution.py:915
  123.4 0.0 copy-done
  123.4 1.3 %add_bitcast_fusion = f32[1,512,768]{2,1,0:T(8,128)} fusion(bf16[512,768]{1,0:T(8,128)(2,1)S(1)} %collective-permute-done.8, f32[512,768]{1,0:T(8,128)S(1)} %copy-done, bf16[512,768]{1,0:T(8,128)(2,1)S(1)} %collective-permute-done.3), kind=kLoop, calls=%fused_computation | loop fusion | flops 1572864 | bytes 4718592 | tf_op jit(solution)/shard_map/reshape | solution.py:1004
  (2 shorter events, 0.0 us)
Async XLA Ops:
  0.6 3.8 %collective-permute-start = (bf16[512,768]{1,0:T(8,128)(2,1)}, bf16[512,768]{1,0:T(8,128)(2,1)}, u32[]{:S(2)}, u32[]{:S(2)}) collective-permute-start(bf16[512,768]{1,0:T(8,128)(2,1)} %bitcast.6), channel_id=1, source_target_pairs={{0,1},{1,0},{2,3},{3,2},{4,5},{5,4},{6,7},{7,6},{8,9},{9,8},{10,11... | collective-permute-start | bytes 2359304 | tf_op jit(solution)/shard_map/ppermute | solution.py:915
  1.2 22.3 %collective-permute-start.1 = (bf16[512,768]{1,0:T(8,128)(2,1)}, bf16[512,768]{1,0:T(8,128)(2,1)}, u32[]{:S(2)}, u32[]{:S(2)}) collective-permute-start(bf16[512,768]{1,0:T(8,128)(2,1)} %bitcast.7), channel_id=1, source_target_pairs={{0,2},{1,3},{2,0},{3,1},{4,6},{5,7},{6,4},{7,5},{8,10},{9,11},{10,... | collective-permute-start | bytes 2359304 | tf_op jit(solution)/shard_map/ppermute | solution.py:915
  23.4 2.7 %collective-permute-start.2 = (bf16[512,768]{1,0:T(8,128)(2,1)}, bf16[512,768]{1,0:T(8,128)(2,1)}, u32[]{:S(2)}, u32[]{:S(2)}) collective-permute-start(bf16[512,768]{1,0:T(8,128)(2,1)} %collective-permute-done.1.x_two_hbm), channel_id=1, source_target_pairs={{0,1},{1,0},{2,3},{3,2},{4,5},{5,4},{6,7},{7,6},{8,9},{9,8},{10,11... | collective-permute-start | bytes 2359304 | tf_op jit(solution)/shard_map/ppermute | solution.py:915
  98.6 6.9 %copy-start.2 = (f32[4,1024]{1,0:T(4,128)S(1)}, f32[4,1024]{1,0:T(4,128)}, u32[]{:S(2)}) copy-start(f32[4,1024]{1,0:T(4,128)} %get-tuple-element.62) | copy-start | bytes 49156
  98.6 24.8 %copy-start = (f32[512,768]{1,0:T(8,128)S(1)}, f32[512,768]{1,0:T(8,128)}, u32[]{:S(2)}) copy-start(f32[512,768]{1,0:T(8,128)} %get-tuple-element.56) | copy-start | bytes 4718596
  98.6 2.7 %collective-permute-start.4 = (bf16[512,768]{1,0:T(8,128)(2,1)}, bf16[512,768]{1,0:T(8,128)(2,1)S(1)}, u32[]{:S(2)}, u32[]{:S(2)}) collective-permute-start(bf16[512,768]{1,0:T(8,128)(2,1)} %get-tuple-element.59), channel_id=1, source_target_pairs={{0,1},{1,0},{2,3},{3,2},{4,5},{5,4},{6,7},{7,6},{8,9},{9,8},{10,11... | collective-permute-start | bytes 2359304 | tf_op jit(solution)/shard_map/ppermute | solution.py:915
  98.8 4.7 %collective-permute-start.7 = (f32[4,1024]{1,0:T(4,128)}, f32[4,1024]{1,0:T(4,128)S(1)}, u32[]{:S(2)}, u32[]{:S(2)}) collective-permute-start(f32[4,1024]{1,0:T(4,128)} %get-tuple-element.62), channel_id=1, source_target_pairs={{0,3},{1,2},{2,1},{3,0},{4,7},{5,6},{6,5},{7,4},{8,11},{9,10},{10,... | collective-permute-start | bytes 49160 | tf_op jit(solution)/shard_map/ppermute | solution.py:915
  100.6 3.9 %collective-permute-start.6 = (f32[4,1024]{1,0:T(4,128)}, f32[4,1024]{1,0:T(4,128)S(1)}, u32[]{:S(2)}, u32[]{:S(2)}) collective-permute-start(f32[4,1024]{1,0:T(4,128)} %get-tuple-element.62), channel_id=1, source_target_pairs={{0,2},{1,3},{2,0},{3,1},{4,6},{5,7},{6,4},{7,5},{8,10},{9,11},{10,... | collective-permute-start | bytes 49160 | tf_op jit(solution)/shard_map/ppermute | solution.py:915
  100.8 3.8 %collective-permute-start.5 = (f32[4,1024]{1,0:T(4,128)}, f32[4,1024]{1,0:T(4,128)S(1)}, u32[]{:S(2)}, u32[]{:S(2)}) collective-permute-start(f32[4,1024]{1,0:T(4,128)} %get-tuple-element.62), channel_id=1, source_target_pairs={{0,1},{1,0},{2,3},{3,2},{4,5},{5,4},{6,7},{7,6},{8,9},{9,8},{10,11... | collective-permute-start | bytes 49160 | tf_op jit(solution)/shard_map/ppermute | solution.py:915
  100.8 18.2 %collective-permute-start.3 = (bf16[512,768]{1,0:T(8,128)(2,1)}, bf16[512,768]{1,0:T(8,128)(2,1)S(1)}, u32[]{:S(2)}, u32[]{:S(2)}) collective-permute-start(bf16[512,768]{1,0:T(8,128)(2,1)} %get-tuple-element.57), channel_id=1, source_target_pairs={{0,1},{1,0},{2,3},{3,2},{4,5},{5,4},{6,7},{7,6},{8,9},{9,8},{10,11... | collective-permute-start | bytes 2359304 | tf_op jit(solution)/shard_map/ppermute | solution.py:915
  104.6 18.8 %collective-permute-start.8 = (bf16[512,768]{1,0:T(8,128)(2,1)}, bf16[512,768]{1,0:T(8,128)(2,1)S(1)}, u32[]{:S(2)}, u32[]{:S(2)}) collective-permute-start(bf16[512,768]{1,0:T(8,128)(2,1)} %add_convert_fusion), channel_id=1, source_target_pairs={{0,2},{1,3},{2,0},{3,1},{4,6},{5,7},{6,4},{7,5},{8,10},{9,11},{10,... | collective-permute-start | bytes 2359304 | tf_op jit(solution)/shard_map/ppermute | solution.py:915
  105.5 4.8 %collective-permute-start.11 = (f32[4,1024]{1,0:T(4,128)S(1)}, f32[4,1024]{1,0:T(4,128)S(1)}, u32[]{:S(2)}, u32[]{:S(2)}) collective-permute-start(f32[4,1024]{1,0:T(4,128)S(1)} %add_add_fusion.1), channel_id=1, source_target_pairs={{0,12},{4,8},{8,4},{12,0},{16,28},{20,24},{24,20},{28,16},{1,13},{... | collective-permute-start | bytes 49160 | tf_op jit(solution)/shard_map/ppermute | solution.py:915
  108.0 3.7 %collective-permute-start.10 = (f32[4,1024]{1,0:T(4,128)S(1)}, f32[4,1024]{1,0:T(4,128)S(1)}, u32[]{:S(2)}, u32[]{:S(2)}) collective-permute-start(f32[4,1024]{1,0:T(4,128)S(1)} %add_add_fusion.1), channel_id=1, source_target_pairs={{0,8},{4,12},{8,0},{12,4},{16,24},{20,28},{24,16},{28,20},{1,9},{5... | collective-permute-start | bytes 49160 | tf_op jit(solution)/shard_map/ppermute | solution.py:915
  108.5 3.7 %collective-permute-start.9 = (f32[4,1024]{1,0:T(4,128)S(1)}, f32[4,1024]{1,0:T(4,128)S(1)}, u32[]{:S(2)}, u32[]{:S(2)}) collective-permute-start(f32[4,1024]{1,0:T(4,128)S(1)} %add_add_fusion.1), channel_id=1, source_target_pairs={{0,4},{4,0},{8,12},{12,8},{16,20},{20,16},{24,28},{28,24},{1,5},{5... | collective-permute-start | bytes 49160 | tf_op jit(solution)/shard_map/ppermute | solution.py:915
  112.2 4.7 %copy-start.1 = (f32[4,1024]{1,0:T(4,128)}, f32[4,1024]{1,0:T(4,128)S(1)}, u32[]{:S(2)}) copy-start(f32[4,1024]{1,0:T(4,128)S(1)} %add_add_fusion.refs_0_) | copy-start | bytes 49156
  112.3 4.7 %collective-permute-start.12 = (f32[4,1024]{1,0:T(4,128)S(1)}, f32[4,1024]{1,0:T(4,128)S(1)}, u32[]{:S(2)}, u32[]{:S(2)}) collective-permute-start(f32[4,1024]{1,0:T(4,128)S(1)} %add_add_fusion.refs_0_), channel_id=1, source_target_pairs={{0,16},{4,20},{8,24},{12,28},{16,0},{20,4},{24,8},{28,12},{1,17},{... | collective-permute-start | bytes 49160 | tf_op jit(solution)/shard_map/ppermute | solution.py:915
  117.0 0.6 copy-start.3

commit v2 on v1

--- a/solution.py
+++ b/solution.py
@@ -137,10 +137,10 @@
         span = span_of(pair, PAIR)
         for half in range(2):
             head = 2 * pair + half
-            q_own = q[:, span] * half_mask(half)
-            for block in range(blocks):
-                scores = product_back(q_own, k[block, :, span])
-                e[head, :, block * rows : (block + 1) * rows] = jnp.exp2(scores).astype(bf16)
+            keys = k[:, :, span].reshape(blocks * rows, PAIR)
+            scores = product_back(q[:, span] * half_mask(half), keys)
+            for at in row_chunks(rows):
+                e[head, at, :] = jnp.exp2(scores[at]).astype(bf16)
             own = span_of(head, HEAD)
             out = product_back(jnp.concatenate([vt[own, :], ones], axis=0), e[head])
             row = pl.ds(head, 1)
@@ -266,6 +266,7 @@
     sems_in,
     sems_out,
     sems_e,
+    sems_o,
 ):
     rows, width = x.shape[1:]
     come = make_copies(
@@ -283,7 +284,7 @@
     for n in (0, 6, 4, 1, 2, 3, 5):
         come[n].start()
     leave = make_copies(
-        ((q, q_hbm), (qt, qt_hbm), (v, v_hbm), (kt, kt_hbm), (w_all, w_all_hbm), (bt, bt_hbm), (o, o_hbm)),
+        ((q, q_hbm), (qt, qt_hbm), (v, v_hbm), (kt, kt_hbm), (w_all, w_all_hbm), (bt, bt_hbm)),
         sems_out,
     )
     l[...] = jnp.ones_like(l)
@@ -335,21 +336,30 @@
         heads = pl.ds(2 * pair, 2)
         return pltpu.make_async_copy(e.at[heads], e_hbm.at[heads], sems_e.at[pair])
 
+    def copy_o(pair):
+        span = span_of(pair, PAIR)
+        return pltpu.make_async_copy(o.at[span], o_hbm.at[span], sems_o.at[pair])
+
+    def send(pair):
+        copy_e(pair).start()
+        copy_o(pair).start()
+
     def restore():
         @pl.when(covered)
         def _():
             for pair in range(width // PAIR):
                 copy_e(pair).wait()
+                copy_o(pair).wait()
 
     safe = attend(
-        covered, q, k, vt, e, o, l, m, m, col, False, starts, count, lambda pair: copy_e(pair).start(), restore
+        covered, q, k, vt, e, o, l, m, m, col, False, starts, count, send, restore
     )
     fast_ref[0] = jnp.where(safe, 1, 0)
-    leave[6].start()
     for copy in leave:
         copy.wait()
     for pair in range(width // PAIR):
         copy_e(pair).wait()
+        copy_o(pair).wait()
 
 
 def near(lengths, d, b, biases, x, w_key, shared_a, shared_b, w_query, w_value, x_one):
@@ -382,7 +392,8 @@
         + buffers((rows, PAIR), dtype=f32)
         + [
             pltpu.SemaphoreType.DMA((7,)),
-            pltpu.SemaphoreType.DMA((7,)),
+            pltpu.SemaphoreType.DMA((6,)),
+            pltpu.SemaphoreType.DMA((width // PAIR,)),
             pltpu.SemaphoreType.DMA((width // PAIR,)),
         ],
         32 * rows * rows * width + 10 * rows * width * width + 4 * width * rank * width,
@@ -395,8 +406,9 @@
     go, got, qt, less, factor, v, kt, e, gqt, gvts, gkvs, scores, ready, done
 ):
     rows, width = go.shape
-    blocks = len(v)
-    lane = lanes((rows, PAIR))
+    blocks = v.shape[0]
+    lane = lanes((blocks * rows, PAIR))
+    row_lane = lanes((rows, PAIR))
 
     def body(pair):
         span = span_of(pair, PAIR)
@@ -406,19 +418,15 @@
             head = 2 * pair + half
             left = jnp.concatenate([go[:, span] * half_mask(half), less[...]], axis=1)
             picks = jnp.where(lane // 2 == head, 1.0, 0.0).astype(bf16)
-            towards = [
-                product_back(left, jnp.concatenate([v[block][:, span], picks], axis=1))
-                for block in range(blocks)
-            ]
-            own = jnp.sum(jnp.where(lane == head, factor[...], 0.0), axis=1, keepdims=True)
+            values = v[:, :, span].reshape(blocks * rows, PAIR)
+            towards = product_back(left, jnp.concatenate([values, picks], axis=1))
+            own = jnp.sum(jnp.where(row_lane == head, factor[...], 0.0), axis=1, keepdims=True)
             own = jnp.broadcast_to(own, (rows, PAIR)).astype(bf16)
-            own = jnp.concatenate([own] * (rows // PAIR), axis=1)
-            for block in range(blocks):
-                here = slice(block * rows, (block + 1) * rows)
-                for at in row_chunks(rows):
-                    weights = e[head, at, here] * own[at]
-                    e[head, at, here] = weights
-                    scores[half, at, here] = weights * towards[block][at].astype(bf16)
+            own = jnp.concatenate([own] * (blocks * rows // PAIR), axis=1)
+            for at in row_chunks(rows):
+                weights = e[head, at, :] * own[at]
+                e[head, at, :] = weights
+                scores[half, at, :] = weights * towards[at].astype(bf16)
             span_own = span_of(head, HEAD)
             g_values.append(product(got[span_own, :], e[head]).astype(bf16))
             g_keys.append((product(qt[span_own, :], scores[half]) * LN2).astype(bf16))
@@ -587,11 +595,12 @@
     bt_hbm,
     total_ref,
     act_hbm,
-    rest_hbm,
+    g_one_hbm,
     two_hbm,
     three_hbm,
     one_hbm,
-    w_all,
+    gq_hbm,
+    wkv,
     x_far,
     q,
     o,
@@ -627,7 +636,7 @@
     go, low_ref = q, x_far.at[1]
     come = make_copies(
         (
-            (w_all_hbm, w_all),
+            (w_all_hbm.at[:, pl.ds(width, 2 * width)], wkv),
             (x_two_hbm, x_far.at[0]),
             (x_three_hbm, x_far.at[1]),
             (q_hbm, q),
@@ -666,8 +675,9 @@
             (cot, act_hbm),
             (x_far.at[0], two_hbm),
             (x_far.at[1], three_hbm),
-            (g_one, rest_hbm),
+            (g_one, g_one_hbm),
             (x_far.at[1], one_hbm),
+            (go, gq_hbm),
         ),
         sems_out,
     )
@@ -679,7 +689,6 @@
     l[...] = l_prev[...]
     m[...] = m_prev[...]
     mb[...] = jnp.zeros_like(mb)
-    wkv = w_all.at[:, pl.ds(width, 2 * width)]
     for copy in come[:3]:
         copy.wait()
     for copy in come[3:]:
@@ -768,7 +777,7 @@
             qt,
             less,
             factors.at[chip],
-            [kv.at[2 * chip + block] for block in range(2)],
+            kv.at[pl.ds(2 * chip, 2)],
             turned.at[chip],
             e,
             o,
@@ -804,9 +813,9 @@
     for at in row_chunks(width):
         got[at, :] = (o[at, :] * HEAD ** (-0.5)).astype(bf16)
     go[...] = got[...].T
-    out = product_back(go[...], w_all[:, 0:width])
+    leave[5].start()
     for at in row_chunks(rows):
-        g_one[at, :] += out[at] + x_far[0, at, :].astype(f32)
+        g_one[at, :] += x_far[0, at, :].astype(f32)
     leave[3].start()
     for copy in late[2:]:
         copy.wait()
@@ -828,7 +837,7 @@
             sums = jnp.sum(part * d_ref[n : n + 1, :], axis=1, keepdims=True)
             total_ref[2 + n : 3 + n, at] = jnp.sum(jnp.where(eye, sums, 0.0), axis=0, keepdims=True)
         total_ref[n : n + 1, :] = for_d
-    for copy in (leave[0], leave[3], leave[4]):
+    for copy in (leave[0], *leave[3:]):
         copy.wait()
 
 
@@ -855,8 +864,9 @@
             (HBM, low, bf16),
             (HBM, low, bf16),
             (HBM, low, bf16),
+            (HBM, low, bf16),
         ],
-        buffers((width, 3 * width), (2,) + low, low)
+        buffers((width, 2 * width), (2,) + low, low)
         + buffers(flat, dtype=f32)
         + buffers(square, (width, hidden), (hidden, width), low, low, flat)
         + buffers(low, dtype=f32)
@@ -871,7 +881,7 @@
             pltpu.SemaphoreType.DMA((11,)),
             pltpu.SemaphoreType.DMA((width // PAIR,)),
             pltpu.SemaphoreType.DMA((8,)),
-            pltpu.SemaphoreType.DMA((5,)),
+            pltpu.SemaphoreType.DMA((6,)),
         ],
         160 * rows * rows * width + 30 * rows * width * width + 8 * rows * width * hidden,
         60 * 1024 * 1024,
@@ -953,7 +963,7 @@
     )
     x_two, o = lax.optimization_barrier((x_two, o))
     x_three = swap(x_two, "seq", seq_size, 1)
-    totals, activations, rest, two, three, one = far(
+    totals, activations, g_one, two, three, one, gq = far(
         (
             lengths,
             fast,
@@ -998,6 +1008,7 @@
     moment_d, second_d, moment_b, second_b, new_d, new_b, copy_d, copy_b = step(
         terms, (scale_d, mom_d, sec_d, scale_b, mom_b, sec_b)
     )
+    rest = lax.optimization_barrier(g_one + product_back(gq, w_all[:, :width]))
     grad_inputs = rest + from_one.astype(f32) + from_two.astype(f32)
     return (
         activations.reshape(tokens.shape),

time: 125 us -> 124 us (level)
  waiting for transfers between devices: 13.2 us -> 10.8 us
  matrix products: 0 us -> 2.2 us
  Pallas kernels: 92.9 us -> 91.4 us
    ppermute x13, waiting for transfers between devices: 13.2 us -> 10.8 us  [swap(): return lax.ppermute(value, axis, [(i, i ^ mask) for i in range(size)])]
    dot_general x0 -> x1, matrix products: none -> 2.2 us  [product_back(): lax.dot_general(left, right, (((1,), (1,)), ((), ())), preferred_element_...]
    pallas_call x2, Pallas kernels: 91.4 us -> 89.9 us  [call(): pl.pallas_call(kernel, in_specs=in_specs, out_specs=[spec for spec, _, _...]
  transfers between devices with their start and end apart: 13 -> 13, of which waited for: 7 -> 6; matrix products, arithmetic and copies ran while one was open for 2% -> 4% of each run, Pallas kernels for 16% -> 16%
where the time goes in v2:
time: 124 us; the launch traced here: 123 us
  Pallas kernels  91.4 us (74%)
  starting transfers between devices  13.1 us (11%)
  waiting for transfers between devices  10.8 us (9%)
  other arithmetic  3.75 us (3%)
  matrix products  2.2 us (2%)
  between operations  1.42 us (1%)
    pallas_call x2, Pallas kernels, call(): pl.pallas_call(kernel, in_specs=in_specs, out_specs=[spec for spec, _, _...  89.9 us
    ppermute x13, starting transfers between devices, swap(): return lax.ppermute(value, axis, [(i, i ^ mask) for i in range(size)])  13.1 us
    ppermute x13, waiting for transfers between devices, swap(): return lax.ppermute(value, axis, [(i, i ^ mask) for i in range(size)])  10.8 us
  transfers between devices with their start and end apart: 13, of which 6 were waited for; matrix products, arithmetic and copies ran while one was open for 4% of the time, Pallas kernels for 16%

profile of v2, /device:TPU:0, one launch (start us, length us, event | category | flops | bytes accessed | tf_op | source)
XLA Modules:
  0.0 123.2 jit_solution(14905966305164583366)
XLA Ops:
  0.6 0.5 collective-permute-start
  1.2 2.6 %collective-permute-start.1 = (bf16[512,768]{1,0:T(8,128)(2,1)}, bf16[512,768]{1,0:T(8,128)(2,1)}, u32[]{:S(2)}, u32[]{:S(2)}) collective-permute-start(bf16[512,768]{1,0:T(8,128)(2,1)} %bitcast.8), channel_id=1, source_target_pairs={{0,2},{1,3},{2,0},{3,1},{4,6},{5,7},{6,4},{7,5},{8,10},{9,11},{10,... | collective-permute-start | bytes 2359304 | tf_op jit(solution)/shard_map/ppermute | solution.py:925
  4.4 0.0 collective-permute-done.x_one_hbm
  4.4 18.6 %near.1 = (s32[1]{0:T(128)}, f32[16,512]{1,0:T(8,128)}, f32[16,512]{1,0:T(8,128)}, bf16[12,512,1024]{2,1,0:T(8,128)(2,1)}, f32[768,512]{1,0:T(8,128)}, /*index=5...) custom-call(s32[1]{0:T(128)S(6)} %copy.30.count_ref, ...), custom_call_target="tpu_custom_call" | custom-call | flops 11878268928 | bytes 41943040 | tf_op jit(solution)/shard_map/near/pallas_call | solution.py:96
  23.0 0.0 collective-permute-done.1.x_two_hbm
  23.0 0.2 collective-permute-start.2
  23.3 2.5 %collective-permute-done.2.x_three_hbm = bf16[512,768]{1,0:T(8,128)(2,1)} collective-permute-done((bf16[512,768]{1,0:T(8,128)(2,1)}, bf16[512,768]{1,0:T(8,128)(2,1)}, u32[]{:S(2)}, u32[]{:S(2)}) %collective-permute-start.2) | collective-permute-done | bytes 786464 | tf_op jit(solution)/shard_map/ppermute | solution.py:925
  25.7 71.3 %far.1 = (f32[4,1024]{1,0:T(4,128)}, bf16[512,768]{1,0:T(8,128)(2,1)}, f32[512,768]{1,0:T(8,128)}, bf16[512,768]{1,0:T(8,128)(2,1)}, bf16[512,768]{1,0:T(8,128)(...) custom-call(s32[1]{0:T(128)S(6)} %copy.30.count_ref, s32[1]{0:T(128)} %get-tuple-element.43.fast_ref, ...), custom_call_target="tpu_custom_call" | custom-call | flops 50935627776 | bytes 62914560 | tf_op jit(solution)/shard_map/far/pallas_call | solution.py:96
  97.1 0.0 copy-start.2
  97.1 0.0 copy-start.4
  97.1 0.2 collective-permute-start.4
  97.3 1.8 %collective-permute-start.7 = (f32[4,1024]{1,0:T(4,128)}, f32[4,1024]{1,0:T(4,128)S(1)}, u32[]{:S(2)}, u32[]{:S(2)}) collective-permute-start(f32[4,1024]{1,0:T(4,128)} %get-tuple-element.64), channel_id=1, source_target_pairs={{0,3},{1,2},{2,1},{3,0},{4,7},{5,6},{6,5},{7,4},{8,11},{9,10},{10,... | collective-permute-start | bytes 49160 | tf_op jit(solution)/shard_map/ppermute | solution.py:925
  99.2 0.1 collective-permute-start.6
  99.3 0.0 collective-permute-start.5
  99.3 0.5 collective-permute-start.3
  99.8 0.0 collective-permute-done.4
  99.8 2.2 %add_convert_fusion = bf16[512,768]{1,0:T(8,128)(2,1)} fusion(bf16[512,768]{1,0:T(8,128)(2,1)S(1)} %collective-permute-done.4, bf16[512,768]{1,0:T(8,128)(2,1)} %get-tuple-element.60), kind=kLoop, calls=%fused_computation.1 | loop fusion | flops 1572864 | bytes 2359296 | tf_op jit(solution)/shard_map/convert_element_type | solution.py:999
  102.0 0.0 collective-permute-done.7
  102.0 1.1 collective-permute-done.6
  103.1 0.0 collective-permute-done.5
  103.1 0.9 collective-permute-start.8
  104.0 0.0 copy-done.2
  104.0 2.6 %collective-permute-start.11 = (f32[4,1024]{1,0:T(4,128)S(1)}, f32[4,1024]{1,0:T(4,128)S(1)}, u32[]{:S(2)}, u32[]{:S(2)}) collective-permute-start(f32[4,1024]{1,0:T(4,128)S(1)} %add_add_fusion.1), channel_id=1, source_target_pairs={{0,12},{4,8},{8,4},{12,0},{16,28},{20,24},{24,20},{28,16},{1,13},{... | collective-permute-start | bytes 49160 | tf_op jit(solution)/shard_map/ppermute | solution.py:925
  106.6 0.4 collective-permute-start.10
  107.0 0.5 collective-permute-start.9
  107.5 1.3 %collective-permute-done.11 = f32[4,1024]{1,0:T(4,128)S(1)} collective-permute-done((f32[4,1024]{1,0:T(4,128)S(1)}, f32[4,1024]{1,0:T(4,128)S(1)}, u32[]{:S(2)}, u32[]{:S(2)}) %collective-permute-start.11) | collective-permute-done | bytes 16416 | tf_op jit(solution)/shard_map/ppermute | solution.py:925
  108.8 1.5 %collective-permute-done.10 = f32[4,1024]{1,0:T(4,128)S(1)} collective-permute-done((f32[4,1024]{1,0:T(4,128)S(1)}, f32[4,1024]{1,0:T(4,128)S(1)}, u32[]{:S(2)}, u32[]{:S(2)}) %collective-permute-start.10) | collective-permute-done | bytes 16416 | tf_op jit(solution)/shard_map/ppermute | solution.py:925
  110.3 0.4 collective-permute-done.9
  110.8 0.0 copy-start.1
  110.8 2.6 %collective-permute-start.12 = (f32[4,1024]{1,0:T(4,128)S(1)}, f32[4,1024]{1,0:T(4,128)S(1)}, u32[]{:S(2)}, u32[]{:S(2)}) collective-permute-start(f32[4,1024]{1,0:T(4,128)S(1)} %add_add_fusion.refs_0_), channel_id=1, source_target_pairs={{0,16},{4,20},{8,24},{12,28},{16,0},{20,4},{24,8},{28,12},{1,17},{... | collective-permute-start | bytes 49160 | tf_op jit(solution)/shard_map/ppermute | solution.py:925
  113.4 0.0 copy-done.4
  113.4 0.0 copy-start
  113.4 2.2 %fusion = f32[512,768]{1,0:T(8,128)S(1)} fusion(bf16[512,768]{1,0:T(8,128)(2,1)S(1)} %copy-done.4, bf16[768,2304]{1,0:T(8,128)(2,1)} %get-tuple-element.46.w_all_hbm), kind=kOutput, calls=%fused_computation.2 | convolution fusion | flops 603979776 | bytes 3538944 | tf_op jit(solution)/shard_map/dot_general | solution.py:38
  115.6 0.0 copy-done.1
  115.6 0.0 copy-done
  115.7 0.2 add.30
  115.9 0.0 collective-permute-done.12.refs_1_
  115.9 0.0 copy-start.3
  115.9 0.6 copy-done.3
  116.5 1.4 %step.1 = (f32[2,1024]{1,0:T(2,128)}, f32[2,1024]{1,0:T(2,128)}, f32[2,768]{1,0:T(2,128)}, f32[2,768]{1,0:T(2,128)}, f32[2,1024]{1,0:T(2,128)}, /*index=5*/f32[2...) custom-call(f32[4,1024]{1,0:T(4,128)} %copy-done.1, f32[4,1024]{1,0:T(4,128)} %copy-done.3, f32[2,1024]{1,0:T(2,128)} %refs_2_.1, ...), custom_call_target="tpu_custom_call" | custom-call | tf_op jit(solution)/shard_map/step/pallas_call | solution.py:915
  117.9 0.0 collective-permute-done.3
  117.9 4.0 %collective-permute-done.8 = bf16[512,768]{1,0:T(8,128)(2,1)S(1)} collective-permute-done((bf16[512,768]{1,0:T(8,128)(2,1)}, bf16[512,768]{1,0:T(8,128)(2,1)S(1)}, u32[]{:S(2)}, u32[]{:S(2)}) %collective-permute-start.8) | collective-permute-done | bytes 786464 | tf_op jit(solution)/shard_map/ppermute | solution.py:925
  121.9 1.3 %add_bitcast_fusion = f32[1,512,768]{2,1,0:T(8,128)} fusion(bf16[512,768]{1,0:T(8,128)(2,1)S(1)} %collective-permute-done.8, f32[512,768]{1,0:T(8,128)S(1)} %add.30, bf16[512,768]{1,0:T(8,128)(2,1)S(1)} %collective-permute-done.3), kind=kLoop, calls=%fused_computation | loop fusion | flops 1572864 | bytes 4718592 | tf_op jit(solution)/shard_map/reshape | solution.py:1015
  (2 shorter events, 0.0 us)
Async XLA Ops:
  0.6 3.8 %collective-permute-start = (bf16[512,768]{1,0:T(8,128)(2,1)}, bf16[512,768]{1,0:T(8,128)(2,1)}, u32[]{:S(2)}, u32[]{:S(2)}) collective-permute-start(bf16[512,768]{1,0:T(8,128)(2,1)} %bitcast.7), channel_id=1, source_target_pairs={{0,1},{1,0},{2,3},{3,2},{4,5},{5,4},{6,7},{7,6},{8,9},{9,8},{10,11... | collective-permute-start | bytes 2359304 | tf_op jit(solution)/shard_map/ppermute | solution.py:925
  1.2 21.9 %collective-permute-start.1 = (bf16[512,768]{1,0:T(8,128)(2,1)}, bf16[512,768]{1,0:T(8,128)(2,1)}, u32[]{:S(2)}, u32[]{:S(2)}) collective-permute-start(bf16[512,768]{1,0:T(8,128)(2,1)} %bitcast.8), channel_id=1, source_target_pairs={{0,2},{1,3},{2,0},{3,1},{4,6},{5,7},{6,4},{7,5},{8,10},{9,11},{10,... | collective-permute-start | bytes 2359304 | tf_op jit(solution)/shard_map/ppermute | solution.py:925
  23.0 2.7 %collective-permute-start.2 = (bf16[512,768]{1,0:T(8,128)(2,1)}, bf16[512,768]{1,0:T(8,128)(2,1)}, u32[]{:S(2)}, u32[]{:S(2)}) collective-permute-start(bf16[512,768]{1,0:T(8,128)(2,1)} %collective-permute-done.1.x_two_hbm), channel_id=1, source_target_pairs={{0,1},{1,0},{2,3},{3,2},{4,5},{5,4},{6,7},{7,6},{8,9},{9,8},{10,11... | collective-permute-start | bytes 2359304 | tf_op jit(solution)/shard_map/ppermute | solution.py:925
  97.1 6.9 %copy-start.2 = (f32[4,1024]{1,0:T(4,128)S(1)}, f32[4,1024]{1,0:T(4,128)}, u32[]{:S(2)}) copy-start(f32[4,1024]{1,0:T(4,128)} %get-tuple-element.64) | copy-start | bytes 49156
  97.1 16.4 %copy-start.4 = (bf16[512,768]{1,0:T(8,128)(2,1)S(1)}, bf16[512,768]{1,0:T(8,128)(2,1)}, u32[]{:S(2)}) copy-start(bf16[512,768]{1,0:T(8,128)(2,1)} %get-tuple-element.58) | copy-start | bytes 2359300
  97.1 2.7 %collective-permute-start.4 = (bf16[512,768]{1,0:T(8,128)(2,1)}, bf16[512,768]{1,0:T(8,128)(2,1)S(1)}, u32[]{:S(2)}, u32[]{:S(2)}) collective-permute-start(bf16[512,768]{1,0:T(8,128)(2,1)} %get-tuple-element.61), channel_id=1, source_target_pairs={{0,1},{1,0},{2,3},{3,2},{4,5},{5,4},{6,7},{7,6},{8,9},{9,8},{10,11... | collective-permute-start | bytes 2359304 | tf_op jit(solution)/shard_map/ppermute | solution.py:925
  97.3 4.7 %collective-permute-start.7 = (f32[4,1024]{1,0:T(4,128)}, f32[4,1024]{1,0:T(4,128)S(1)}, u32[]{:S(2)}, u32[]{:S(2)}) collective-permute-start(f32[4,1024]{1,0:T(4,128)} %get-tuple-element.64), channel_id=1, source_target_pairs={{0,3},{1,2},{2,1},{3,0},{4,7},{5,6},{6,5},{7,4},{8,11},{9,10},{10,... | collective-permute-start | bytes 49160 | tf_op jit(solution)/shard_map/ppermute | solution.py:925
  99.2 3.9 %collective-permute-start.6 = (f32[4,1024]{1,0:T(4,128)}, f32[4,1024]{1,0:T(4,128)S(1)}, u32[]{:S(2)}, u32[]{:S(2)}) collective-permute-start(f32[4,1024]{1,0:T(4,128)} %get-tuple-element.64), channel_id=1, source_target_pairs={{0,2},{1,3},{2,0},{3,1},{4,6},{5,7},{6,4},{7,5},{8,10},{9,11},{10,... | collective-permute-start | bytes 49160 | tf_op jit(solution)/shard_map/ppermute | solution.py:925
  99.3 3.8 %collective-permute-start.5 = (f32[4,1024]{1,0:T(4,128)}, f32[4,1024]{1,0:T(4,128)S(1)}, u32[]{:S(2)}, u32[]{:S(2)}) collective-permute-start(f32[4,1024]{1,0:T(4,128)} %get-tuple-element.64), channel_id=1, source_target_pairs={{0,1},{1,0},{2,3},{3,2},{4,5},{5,4},{6,7},{7,6},{8,9},{9,8},{10,11... | collective-permute-start | bytes 49160 | tf_op jit(solution)/shard_map/ppermute | solution.py:925
  99.3 18.6 %collective-permute-start.3 = (bf16[512,768]{1,0:T(8,128)(2,1)}, bf16[512,768]{1,0:T(8,128)(2,1)S(1)}, u32[]{:S(2)}, u32[]{:S(2)}) collective-permute-start(bf16[512,768]{1,0:T(8,128)(2,1)} %get-tuple-element.59), channel_id=1, source_target_pairs={{0,1},{1,0},{2,3},{3,2},{4,5},{5,4},{6,7},{7,6},{8,9},{9,8},{10,11... | collective-permute-start | bytes 2359304 | tf_op jit(solution)/shard_map/ppermute | solution.py:925
  103.1 18.8 %collective-permute-start.8 = (bf16[512,768]{1,0:T(8,128)(2,1)}, bf16[512,768]{1,0:T(8,128)(2,1)S(1)}, u32[]{:S(2)}, u32[]{:S(2)}) collective-permute-start(bf16[512,768]{1,0:T(8,128)(2,1)} %add_convert_fusion), channel_id=1, source_target_pairs={{0,2},{1,3},{2,0},{3,1},{4,6},{5,7},{6,4},{7,5},{8,10},{9,11},{10,... | collective-permute-start | bytes 2359304 | tf_op jit(solution)/shard_map/ppermute | solution.py:925
  104.0 4.8 %collective-permute-start.11 = (f32[4,1024]{1,0:T(4,128)S(1)}, f32[4,1024]{1,0:T(4,128)S(1)}, u32[]{:S(2)}, u32[]{:S(2)}) collective-permute-start(f32[4,1024]{1,0:T(4,128)S(1)} %add_add_fusion.1), channel_id=1, source_target_pairs={{0,12},{4,8},{8,4},{12,0},{16,28},{20,24},{24,20},{28,16},{1,13},{... | collective-permute-start | bytes 49160 | tf_op jit(solution)/shard_map/ppermute | solution.py:925
  106.6 3.7 %collective-permute-start.10 = (f32[4,1024]{1,0:T(4,128)S(1)}, f32[4,1024]{1,0:T(4,128)S(1)}, u32[]{:S(2)}, u32[]{:S(2)}) collective-permute-start(f32[4,1024]{1,0:T(4,128)S(1)} %add_add_fusion.1), channel_id=1, source_target_pairs={{0,8},{4,12},{8,0},{12,4},{16,24},{20,28},{24,16},{28,20},{1,9},{5... | collective-permute-start | bytes 49160 | tf_op jit(solution)/shard_map/ppermute | solution.py:925
  107.0 3.7 %collective-permute-start.9 = (f32[4,1024]{1,0:T(4,128)S(1)}, f32[4,1024]{1,0:T(4,128)S(1)}, u32[]{:S(2)}, u32[]{:S(2)}) collective-permute-start(f32[4,1024]{1,0:T(4,128)S(1)} %add_add_fusion.1), channel_id=1, source_target_pairs={{0,4},{4,0},{8,12},{12,8},{16,20},{20,16},{24,28},{28,24},{1,5},{5... | collective-permute-start | bytes 49160 | tf_op jit(solution)/shard_map/ppermute | solution.py:925
  110.8 4.9 %copy-start.1 = (f32[4,1024]{1,0:T(4,128)}, f32[4,1024]{1,0:T(4,128)S(1)}, u32[]{:S(2)}) copy-start(f32[4,1024]{1,0:T(4,128)S(1)} %add_add_fusion.refs_0_) | copy-start | bytes 49156
  110.8 5.1 %collective-permute-start.12 = (f32[4,1024]{1,0:T(4,128)S(1)}, f32[4,1024]{1,0:T(4,128)S(1)}, u32[]{:S(2)}, u32[]{:S(2)}) collective-permute-start(f32[4,1024]{1,0:T(4,128)S(1)} %add_add_fusion.refs_0_), channel_id=1, source_target_pairs={{0,16},{4,20},{8,24},{12,28},{16,0},{20,4},{24,8},{28,12},{1,17},{... | collective-permute-start | bytes 49160 | tf_op jit(solution)/shard_map/ppermute | solution.py:925
  113.4 2.2 %copy-start = (f32[512,768]{1,0:T(8,128)S(1)}, f32[512,768]{1,0:T(8,128)}, u32[]{:S(2)}) copy-start(f32[512,768]{1,0:T(8,128)} %get-tuple-element.57) | copy-start | bytes 4718596
  115.9 0.6 copy-start.3
